TPU v7x, 256 devices: a whole 4x4x8 slice. The times are simulated.
256 devices in a mesh: gx: 8 (over x, z_lo), gy: 32 (over z_hi, y, core).
Axes of the slice: x: 4, y: 4, z: 8 (z_hi: 4, z_lo: 2; z = z_hi * 2 + z_lo), core: 2. Of those that a mesh axis runs over, the one named last changes fastest.
Arguments:
- filtered: float32 [64, 2048, 1024], P(None, 'gy', 'gx'), may hold values from 0 to 1
- upstream: float32 [64, 2048, 1024], P(None, 'gy', 'gx'), may hold values from -24 to 24
- radius_map: int32 [64, 2048, 1024], P(None, 'gy', 'gx'), may hold values from 2 to 12, as said below
- brick_class: int32 [8, 32], P('gx', 'gy'), may hold values from 2 to 12, as said below
- sharpness: float32 [1], replicated, may hold values from 4 to 16
- threshold: float32 [1], replicated, may hold values from 0.35 to 0.65
Outputs:
- sensitivity: float32 [64, 2048, 1024], P(None, 'gy', 'gx')
Inputs may be any that keep to these rules, and one draw needn't show every extreme that they name: `radius_map`: each brick holds a cell whose radius equals its brick's brick_class. `brick_class`: some brick has class 12.
All inputs are finite; a program needn't handle non-finite values.
Results may differ from a plain program's by a relative error of at most 0.0001.
Values sent between devices are 32-bit elements; how exact they have to be, the bound alone decides.
No kernel may reach another device: no remote copies, remote signals or barrier semaphores. Data moves between devices by JAX's collectives and lax.ppermute only.
A program may use at most 128 MiB of HBM per device.

v0:
```python
import jax
import jax.numpy as jnp
from jax import lax
from jax.sharding import PartitionSpec as P

RMAX = 12


def from_behind(shard, axis, by):
    length = lax.axis_size(axis)
    pairs = [(i, i + by) for i in range(length) if 0 <= i + by < length]
    return lax.ppermute(shard, axis, pairs)


def span_sum(radius, position, extent):
    short_low = jnp.maximum(0, radius - 1 - position)
    short_high = jnp.maximum(0, radius - extent + position)
    whole = radius * radius - short_low * (short_low + 1) // 2 - short_high * (short_high + 1) // 2
    return whole.astype(jnp.float32)


def band(radius, count_rows, count_cols, offset):
    row_index = lax.broadcasted_iota(jnp.int32, (count_rows, count_cols), 0)
    col_index = lax.broadcasted_iota(jnp.int32, (count_rows, count_cols), 1)
    return jnp.maximum(0, radius - jnp.abs(col_index - offset - row_index)).astype(jnp.float32)


def per_device(filtered, upstream, radius_map, brick_class, sharpness, threshold):
    cells_z, cells_y, cells_x = filtered.shape
    margin = RMAX - 1
    highest = lax.Precision.HIGHEST
    reach = jnp.minimum(radius_map, brick_class[0, 0])
    z_index = lax.broadcasted_iota(jnp.int32, reach.shape, 0)
    y_index = lax.broadcasted_iota(jnp.int32, reach.shape, 1) + lax.axis_index("gy") * cells_y
    x_index = lax.broadcasted_iota(jnp.int32, reach.shape, 2) + lax.axis_index("gx") * cells_x
    extent_x = cells_x * lax.axis_size("gx")
    extent_y = cells_y * lax.axis_size("gy")
    weight_sum = (
        span_sum(reach, x_index, extent_x)
        * span_sum(reach, y_index, extent_y)
        * span_sum(reach, z_index, cells_z)
    )
    steepness = sharpness[0]
    centre = threshold[0]
    tangent = jnp.tanh(steepness * (filtered - centre))
    slope = (
        upstream
        * steepness
        * (1.0 - tangent * tangent)
        / (jnp.tanh(steepness * centre) + jnp.tanh(steepness * (1.0 - centre)))
    )
    source = slope / weight_sum
    wide_x = cells_x + 2 * margin
    wide_y = cells_y + 2 * margin

    def spread_class(radius, running):
        masked = jnp.where(reach == radius, source, jnp.zeros_like(source))
        along_x = jnp.einsum(
            "zyx,xX->zyX", masked, band(radius, cells_x, wide_x, margin), precision=highest
        )
        along_y = jnp.einsum(
            "zyX,yY->zYX", along_x, band(radius, cells_y, wide_y, margin), precision=highest
        )
        along_z = jnp.einsum(
            "zYX,zw->wYX", along_y, band(radius, cells_z, cells_z, 0), precision=highest
        )
        return running + along_z

    upper_class = RMAX + 1
    extended = lax.fori_loop(
        2, upper_class, spread_class, jnp.zeros((cells_z, wide_y, wide_x), jnp.float32)
    )
    from_lower = from_behind(extended[:, :, cells_x + margin :], "gx", 1)
    from_upper = from_behind(extended[:, :, :margin], "gx", -1)
    interior = extended[:, :, margin : margin + cells_x]
    interior = (
        interior.at[:, :, :margin].add(from_lower).at[:, :, cells_x - margin :].add(from_upper)
    )
    below = from_behind(interior[:, cells_y + margin :, :], "gy", 1)
    above = from_behind(interior[:, :margin, :], "gy", -1)
    result = interior[:, margin : margin + cells_y, :]
    result = result.at[:, :margin, :].add(below).at[:, cells_y - margin :, :].add(above)
    return result


def solution(mesh):
    return jax.shard_map(
        per_device,
        mesh=mesh,
        in_specs=(
            P(None, "gy", "gx"),
            P(None, "gy", "gx"),
            P(None, "gy", "gx"),
            P("gx", "gy"),
            P(),
            P(),
        ),
        out_specs=P(None, "gy", "gx"),
        check_vma=False,
    )
```

profile of v0, /device:TPU:91, one launch (start us, length us, event | category | flops | bytes accessed | tf_op | source)
XLA Modules:
  0.0 437.2 jit_solution(6657639587606423358)
XLA Ops:
  2.1 13.1 %fusion.50 = (f32[64,64,128]{2,1,0:T(8,128)S(1)}, s32[64,64,128]{2,1,0:T(8,128)}) fusion(f32[64,64,128]{2,1,0:T(8,128)} %param.16, f32[64,64,128]{2,1,0:T(8,128)} %param.17, s32[64]{0:T(128)S(1)} %iota_add_fusion.2, s32[128]{0:T(128)S(1)} %iota_add_fusion.3, f32[]{:T(128)S(6)} %add.136, f32[]{:T(128)} %bitcast.29, f32[]{:T(128)} %bitcast.26, ...), kind=kLoop, calls=%fused_computation.84 | loop fusion | flops 72876032 | bytes 10486544 | tf_op jit(solution)/shard_map/div | solution.py:52
  15.2 291.0 %while.21 = (s32[]{:T(128)}, f32[64,86,150]{1,0,2:T(8,128)}, s32[64,64,128]{2,1,0:T(8,128)}, f32[64,64,128]{2,1,0:T(8,128)S(1)}, s32[]{:T(128)}, /*index=5*/s32[]{:T(128)}, s32[]{:T(128)}) while((s32[]{:T(128)}, f32[64,86,150]{1,0,2:T(8,128)}, s32[64,64,128]{2,1,0:T(8,128)}, f32[64,64,128]{2,1,0:T(8,128)S(1)}, s32[]{:T(128)}, ...), condition=%wide.region_1.2_spmd.clone, body=%wide.region_0.1_spmd.clone.sunk | while | flops 2214683904 | bytes 50276384 | solution.py:70
  20.8 10.1 %convolution_bitcast_fusion.2 = f32[64,86,150]{1,2,0:T(8,128)S(1)} fusion(f32[64,64,150]{2,1,0:T(8,128)S(1)} %fusion.85, s32[86]{0:T(128)S(1)} %iota_add_fusion.7, s32[]{:T(128)S(6)} %add.200), kind=kOutput, calls=%fused_computation.3.clone.1 | convolution fusion | flops 634088320 | bytes 5760348 | tf_op jit(solution)/shard_map/while/body/eval_jaxpr/zyX,yY->zYX/dot_general | solution.py:61
  30.9 8.0 %select_add_fusion.2 = f32[64,86,150]{1,0,2:T(8,128)S(1)} fusion(f32[64,86,150]{1,0,2:T(8,128)S(1)} %bitcast.33, pred[]{:T(512)S(6)} %compare.37, f32[64,86,150]{1,2,0:T(8,128)S(1)} %convolution_bitcast_fusion.2, s32[]{:T(128)S(6)} %add.200), kind=kOutput, calls=%fused_computation.2.clone.1 | convolution fusion | flops 635732480 | bytes 9907205 | tf_op jit(solution)/shard_map/while/body/eval_jaxpr/zYX,zw->wYX/dot_general | solution.py:64
  46.5 10.1 %convolution_bitcast_fusion.2 = f32[64,86,150]{1,2,0:T(8,128)S(1)} fusion(f32[64,64,150]{2,1,0:T(8,128)S(1)} %fusion.85, s32[86]{0:T(128)S(1)} %iota_add_fusion.7, s32[]{:T(128)S(6)} %add.200), kind=kOutput, calls=%fused_computation.3.clone.1 | convolution fusion | flops 634088320 | bytes 5760348 | tf_op jit(solution)/shard_map/while/body/eval_jaxpr/zyX,yY->zYX/dot_general | solution.py:61
  56.6 8.0 %select_add_fusion.2 = f32[64,86,150]{1,0,2:T(8,128)S(1)} fusion(f32[64,86,150]{1,0,2:T(8,128)S(1)} %bitcast.33, pred[]{:T(512)S(6)} %compare.37, f32[64,86,150]{1,2,0:T(8,128)S(1)} %convolution_bitcast_fusion.2, s32[]{:T(128)S(6)} %add.200), kind=kOutput, calls=%fused_computation.2.clone.1 | convolution fusion | flops 635732480 | bytes 9907205 | tf_op jit(solution)/shard_map/while/body/eval_jaxpr/zYX,zw->wYX/dot_general | solution.py:64
  72.1 10.1 %convolution_bitcast_fusion.2 = f32[64,86,150]{1,2,0:T(8,128)S(1)} fusion(f32[64,64,150]{2,1,0:T(8,128)S(1)} %fusion.85, s32[86]{0:T(128)S(1)} %iota_add_fusion.7, s32[]{:T(128)S(6)} %add.200), kind=kOutput, calls=%fused_computation.3.clone.1 | convolution fusion | flops 634088320 | bytes 5760348 | tf_op jit(solution)/shard_map/while/body/eval_jaxpr/zyX,yY->zYX/dot_general | solution.py:61
  82.2 8.0 %select_add_fusion.2 = f32[64,86,150]{1,0,2:T(8,128)S(1)} fusion(f32[64,86,150]{1,0,2:T(8,128)S(1)} %bitcast.33, pred[]{:T(512)S(6)} %compare.37, f32[64,86,150]{1,2,0:T(8,128)S(1)} %convolution_bitcast_fusion.2, s32[]{:T(128)S(6)} %add.200), kind=kOutput, calls=%fused_computation.2.clone.1 | convolution fusion | flops 635732480 | bytes 9907205 | tf_op jit(solution)/shard_map/while/body/eval_jaxpr/zYX,zw->wYX/dot_general | solution.py:64
  97.7 10.1 %convolution_bitcast_fusion.2 = f32[64,86,150]{1,2,0:T(8,128)S(1)} fusion(f32[64,64,150]{2,1,0:T(8,128)S(1)} %fusion.85, s32[86]{0:T(128)S(1)} %iota_add_fusion.7, s32[]{:T(128)S(6)} %add.200), kind=kOutput, calls=%fused_computation.3.clone.1 | convolution fusion | flops 634088320 | bytes 5760348 | tf_op jit(solution)/shard_map/while/body/eval_jaxpr/zyX,yY->zYX/dot_general | solution.py:61
  107.8 8.0 %select_add_fusion.2 = f32[64,86,150]{1,0,2:T(8,128)S(1)} fusion(f32[64,86,150]{1,0,2:T(8,128)S(1)} %bitcast.33, pred[]{:T(512)S(6)} %compare.37, f32[64,86,150]{1,2,0:T(8,128)S(1)} %convolution_bitcast_fusion.2, s32[]{:T(128)S(6)} %add.200), kind=kOutput, calls=%fused_computation.2.clone.1 | convolution fusion | flops 635732480 | bytes 9907205 | tf_op jit(solution)/shard_map/while/body/eval_jaxpr/zYX,zw->wYX/dot_general | solution.py:64
  123.4 10.1 %convolution_bitcast_fusion.2 = f32[64,86,150]{1,2,0:T(8,128)S(1)} fusion(f32[64,64,150]{2,1,0:T(8,128)S(1)} %fusion.85, s32[86]{0:T(128)S(1)} %iota_add_fusion.7, s32[]{:T(128)S(6)} %add.200), kind=kOutput, calls=%fused_computation.3.clone.1 | convolution fusion | flops 634088320 | bytes 5760348 | tf_op jit(solution)/shard_map/while/body/eval_jaxpr/zyX,yY->zYX/dot_general | solution.py:61
  133.5 8.0 %select_add_fusion.2 = f32[64,86,150]{1,0,2:T(8,128)S(1)} fusion(f32[64,86,150]{1,0,2:T(8,128)S(1)} %bitcast.33, pred[]{:T(512)S(6)} %compare.37, f32[64,86,150]{1,2,0:T(8,128)S(1)} %convolution_bitcast_fusion.2, s32[]{:T(128)S(6)} %add.200), kind=kOutput, calls=%fused_computation.2.clone.1 | convolution fusion | flops 635732480 | bytes 9907205 | tf_op jit(solution)/shard_map/while/body/eval_jaxpr/zYX,zw->wYX/dot_general | solution.py:64
  149.0 10.1 %convolution_bitcast_fusion.2 = f32[64,86,150]{1,2,0:T(8,128)S(1)} fusion(f32[64,64,150]{2,1,0:T(8,128)S(1)} %fusion.85, s32[86]{0:T(128)S(1)} %iota_add_fusion.7, s32[]{:T(128)S(6)} %add.200), kind=kOutput, calls=%fused_computation.3.clone.1 | convolution fusion | flops 634088320 | bytes 5760348 | tf_op jit(solution)/shard_map/while/body/eval_jaxpr/zyX,yY->zYX/dot_general | solution.py:61
  159.1 8.0 %select_add_fusion.2 = f32[64,86,150]{1,0,2:T(8,128)S(1)} fusion(f32[64,86,150]{1,0,2:T(8,128)S(1)} %bitcast.33, pred[]{:T(512)S(6)} %compare.37, f32[64,86,150]{1,2,0:T(8,128)S(1)} %convolution_bitcast_fusion.2, s32[]{:T(128)S(6)} %add.200), kind=kOutput, calls=%fused_computation.2.clone.1 | convolution fusion | flops 635732480 | bytes 9907205 | tf_op jit(solution)/shard_map/while/body/eval_jaxpr/zYX,zw->wYX/dot_general | solution.py:64
  174.7 10.1 %convolution_bitcast_fusion.2 = f32[64,86,150]{1,2,0:T(8,128)S(1)} fusion(f32[64,64,150]{2,1,0:T(8,128)S(1)} %fusion.85, s32[86]{0:T(128)S(1)} %iota_add_fusion.7, s32[]{:T(128)S(6)} %add.200), kind=kOutput, calls=%fused_computation.3.clone.1 | convolution fusion | flops 634088320 | bytes 5760348 | tf_op jit(solution)/shard_map/while/body/eval_jaxpr/zyX,yY->zYX/dot_general | solution.py:61
  184.8 8.0 %select_add_fusion.2 = f32[64,86,150]{1,0,2:T(8,128)S(1)} fusion(f32[64,86,150]{1,0,2:T(8,128)S(1)} %bitcast.33, pred[]{:T(512)S(6)} %compare.37, f32[64,86,150]{1,2,0:T(8,128)S(1)} %convolution_bitcast_fusion.2, s32[]{:T(128)S(6)} %add.200), kind=kOutput, calls=%fused_computation.2.clone.1 | convolution fusion | flops 635732480 | bytes 9907205 | tf_op jit(solution)/shard_map/while/body/eval_jaxpr/zYX,zw->wYX/dot_general | solution.py:64
  200.3 10.1 %convolution_bitcast_fusion.2 = f32[64,86,150]{1,2,0:T(8,128)S(1)} fusion(f32[64,64,150]{2,1,0:T(8,128)S(1)} %fusion.85, s32[86]{0:T(128)S(1)} %iota_add_fusion.7, s32[]{:T(128)S(6)} %add.200), kind=kOutput, calls=%fused_computation.3.clone.1 | convolution fusion | flops 634088320 | bytes 5760348 | tf_op jit(solution)/shard_map/while/body/eval_jaxpr/zyX,yY->zYX/dot_general | solution.py:61
  210.4 8.0 %select_add_fusion.2 = f32[64,86,150]{1,0,2:T(8,128)S(1)} fusion(f32[64,86,150]{1,0,2:T(8,128)S(1)} %bitcast.33, pred[]{:T(512)S(6)} %compare.37, f32[64,86,150]{1,2,0:T(8,128)S(1)} %convolution_bitcast_fusion.2, s32[]{:T(128)S(6)} %add.200), kind=kOutput, calls=%fused_computation.2.clone.1 | convolution fusion | flops 635732480 | bytes 9907205 | tf_op jit(solution)/shard_map/while/body/eval_jaxpr/zYX,zw->wYX/dot_general | solution.py:64
  225.9 10.1 %convolution_bitcast_fusion.2 = f32[64,86,150]{1,2,0:T(8,128)S(1)} fusion(f32[64,64,150]{2,1,0:T(8,128)S(1)} %fusion.85, s32[86]{0:T(128)S(1)} %iota_add_fusion.7, s32[]{:T(128)S(6)} %add.200), kind=kOutput, calls=%fused_computation.3.clone.1 | convolution fusion | flops 634088320 | bytes 5760348 | tf_op jit(solution)/shard_map/while/body/eval_jaxpr/zyX,yY->zYX/dot_general | solution.py:61
  251.6 10.1 %convolution_bitcast_fusion.2 = f32[64,86,150]{1,2,0:T(8,128)S(1)} fusion(f32[64,64,150]{2,1,0:T(8,128)S(1)} %fusion.85, s32[86]{0:T(128)S(1)} %iota_add_fusion.7, s32[]{:T(128)S(6)} %add.200), kind=kOutput, calls=%fused_computation.3.clone.1 | convolution fusion | flops 634088320 | bytes 5760348 | tf_op jit(solution)/shard_map/while/body/eval_jaxpr/zyX,yY->zYX/dot_general | solution.py:61
  277.2 10.1 %convolution_bitcast_fusion.2 = f32[64,86,150]{1,2,0:T(8,128)S(1)} fusion(f32[64,64,150]{2,1,0:T(8,128)S(1)} %fusion.85, s32[86]{0:T(128)S(1)} %iota_add_fusion.7, s32[]{:T(128)S(6)} %add.200), kind=kOutput, calls=%fused_computation.3.clone.1 | convolution fusion | flops 634088320 | bytes 5760348 | tf_op jit(solution)/shard_map/while/body/eval_jaxpr/zyX,yY->zYX/dot_general | solution.py:61
  339.3 8.1 %collective-permute-start.2 = (f32[64,11,128]{2,0,1:T(8,128)S(1)}, f32[64,11,128]{2,0,1:T(8,128)S(1)}, u32[]{:S(2)}, u32[]{:S(2)}) collective-permute-start(f32[64,11,128]{2,0,1:T(8,128)S(1)} %copy.13), channel_id=1, source_target_pairs={{0,1},{1,2},{2,3},{3,4},{4,5},{5,6},{6,7},{7,8},{8,9},{9,10},{10,1... | collective-permute-start | bytes 1081352 | tf_op jit(solution)/shard_map/ppermute | solution.py:12
  369.8 20.4 %scatter-add.16 = f32[64,64,128]{1,0,2:T(8,128)} dynamic-update-slice(f32[64,64,128]{1,0,2:T(8,128)} %slice.127, f32[64,11,128]{1,0,2:T(8,128)} %slice_add_fusion.1, s32[]{:T(128)} %constant.224.clone.1, s32[]{:T(128)} %constant.224.clone.1, s32[]{:T(128)} %constant.224.clone.1) | dynamic-update-slice | bytes 720900 | tf_op jit(solution)/shard_map/scatter-add | solution.py:82
  401.5 31.0 %scatter-add.19 = f32[64,64,128]{1,0,2:T(8,128)} dynamic-update-slice(f32[64,64,128]{1,0,2:T(8,128)} %scatter-add.16, f32[64,11,128]{1,0,2:T(8,128)} %slice_add_fusion, s32[]{:T(128)} %constant.224.clone.1, s32[]{:T(128)} %constant.238.clone.1, s32[]{:T(128)} %constant.224.clone.1) | dynamic-update-slice | bytes 720900 | tf_op jit(solution)/shard_map/scatter-add | solution.py:82
  (138 shorter events, 177.8 us)
Async XLA Ops:
  15.5 15.4 %slice-start = ((s8[4915200]{0:T(1024)(128)(4,1)}), s8[4194304]{0:T(1024)(128)(4,1)S(1)}, s32[]{:S(2)}) async-start(s8[4915200]{0:T(1024)(128)(4,1)} %bitcast.32), calls=%async_computation | async-start | bytes 8388608 | tf_op jit(solution)/shard_map/while
  20.8 10.1 %slice-start.1 = ((s8[4915200]{0:T(1024)(128)(4,1)}), s8[720896]{0:T(1024)(128)(4,1)S(1)}, s32[]{:S(2)}) async-start(s8[4915200]{0:T(1024)(128)(4,1)} %bitcast.32), calls=%async_computation.1 | async-start | bytes 1441792 | tf_op jit(solution)/shard_map/while
  41.2 15.4 %slice-start = ((s8[4915200]{0:T(1024)(128)(4,1)}), s8[4194304]{0:T(1024)(128)(4,1)S(1)}, s32[]{:S(2)}) async-start(s8[4915200]{0:T(1024)(128)(4,1)} %bitcast.32), calls=%async_computation | async-start | bytes 8388608 | tf_op jit(solution)/shard_map/while
  46.4 10.1 %slice-start.1 = ((s8[4915200]{0:T(1024)(128)(4,1)}), s8[720896]{0:T(1024)(128)(4,1)S(1)}, s32[]{:S(2)}) async-start(s8[4915200]{0:T(1024)(128)(4,1)} %bitcast.32), calls=%async_computation.1 | async-start | bytes 1441792 | tf_op jit(solution)/shard_map/while
  66.8 15.4 %slice-start = ((s8[4915200]{0:T(1024)(128)(4,1)}), s8[4194304]{0:T(1024)(128)(4,1)S(1)}, s32[]{:S(2)}) async-start(s8[4915200]{0:T(1024)(128)(4,1)} %bitcast.32), calls=%async_computation | async-start | bytes 8388608 | tf_op jit(solution)/shard_map/while
  72.1 10.1 %slice-start.1 = ((s8[4915200]{0:T(1024)(128)(4,1)}), s8[720896]{0:T(1024)(128)(4,1)S(1)}, s32[]{:S(2)}) async-start(s8[4915200]{0:T(1024)(128)(4,1)} %bitcast.32), calls=%async_computation.1 | async-start | bytes 1441792 | tf_op jit(solution)/shard_map/while
  92.4 15.4 %slice-start = ((s8[4915200]{0:T(1024)(128)(4,1)}), s8[4194304]{0:T(1024)(128)(4,1)S(1)}, s32[]{:S(2)}) async-start(s8[4915200]{0:T(1024)(128)(4,1)} %bitcast.32), calls=%async_computation | async-start | bytes 8388608 | tf_op jit(solution)/shard_map/while
  97.7 10.1 %slice-start.1 = ((s8[4915200]{0:T(1024)(128)(4,1)}), s8[720896]{0:T(1024)(128)(4,1)S(1)}, s32[]{:S(2)}) async-start(s8[4915200]{0:T(1024)(128)(4,1)} %bitcast.32), calls=%async_computation.1 | async-start | bytes 1441792 | tf_op jit(solution)/shard_map/while
  118.1 15.4 %slice-start = ((s8[4915200]{0:T(1024)(128)(4,1)}), s8[4194304]{0:T(1024)(128)(4,1)S(1)}, s32[]{:S(2)}) async-start(s8[4915200]{0:T(1024)(128)(4,1)} %bitcast.32), calls=%async_computation | async-start | bytes 8388608 | tf_op jit(solution)/shard_map/while
  123.4 10.1 %slice-start.1 = ((s8[4915200]{0:T(1024)(128)(4,1)}), s8[720896]{0:T(1024)(128)(4,1)S(1)}, s32[]{:S(2)}) async-start(s8[4915200]{0:T(1024)(128)(4,1)} %bitcast.32), calls=%async_computation.1 | async-start | bytes 1441792 | tf_op jit(solution)/shard_map/while
  143.7 15.4 %slice-start = ((s8[4915200]{0:T(1024)(128)(4,1)}), s8[4194304]{0:T(1024)(128)(4,1)S(1)}, s32[]{:S(2)}) async-start(s8[4915200]{0:T(1024)(128)(4,1)} %bitcast.32), calls=%async_computation | async-start | bytes 8388608 | tf_op jit(solution)/shard_map/while
  149.0 10.1 %slice-start.1 = ((s8[4915200]{0:T(1024)(128)(4,1)}), s8[720896]{0:T(1024)(128)(4,1)S(1)}, s32[]{:S(2)}) async-start(s8[4915200]{0:T(1024)(128)(4,1)} %bitcast.32), calls=%async_computation.1 | async-start | bytes 1441792 | tf_op jit(solution)/shard_map/while
  169.4 15.4 %slice-start = ((s8[4915200]{0:T(1024)(128)(4,1)}), s8[4194304]{0:T(1024)(128)(4,1)S(1)}, s32[]{:S(2)}) async-start(s8[4915200]{0:T(1024)(128)(4,1)} %bitcast.32), calls=%async_computation | async-start | bytes 8388608 | tf_op jit(solution)/shard_map/while
  174.7 10.1 %slice-start.1 = ((s8[4915200]{0:T(1024)(128)(4,1)}), s8[720896]{0:T(1024)(128)(4,1)S(1)}, s32[]{:S(2)}) async-start(s8[4915200]{0:T(1024)(128)(4,1)} %bitcast.32), calls=%async_computation.1 | async-start | bytes 1441792 | tf_op jit(solution)/shard_map/while
  195.0 15.4 %slice-start = ((s8[4915200]{0:T(1024)(128)(4,1)}), s8[4194304]{0:T(1024)(128)(4,1)S(1)}, s32[]{:S(2)}) async-start(s8[4915200]{0:T(1024)(128)(4,1)} %bitcast.32), calls=%async_computation | async-start | bytes 8388608 | tf_op jit(solution)/shard_map/while
  200.3 10.1 %slice-start.1 = ((s8[4915200]{0:T(1024)(128)(4,1)}), s8[720896]{0:T(1024)(128)(4,1)S(1)}, s32[]{:S(2)}) async-start(s8[4915200]{0:T(1024)(128)(4,1)} %bitcast.32), calls=%async_computation.1 | async-start | bytes 1441792 | tf_op jit(solution)/shard_map/while
  220.7 15.4 %slice-start = ((s8[4915200]{0:T(1024)(128)(4,1)}), s8[4194304]{0:T(1024)(128)(4,1)S(1)}, s32[]{:S(2)}) async-start(s8[4915200]{0:T(1024)(128)(4,1)} %bitcast.32), calls=%async_computation | async-start | bytes 8388608 | tf_op jit(solution)/shard_map/while
  225.9 10.1 %slice-start.1 = ((s8[4915200]{0:T(1024)(128)(4,1)}), s8[720896]{0:T(1024)(128)(4,1)S(1)}, s32[]{:S(2)}) async-start(s8[4915200]{0:T(1024)(128)(4,1)} %bitcast.32), calls=%async_computation.1 | async-start | bytes 1441792 | tf_op jit(solution)/shard_map/while
  246.3 15.4 %slice-start = ((s8[4915200]{0:T(1024)(128)(4,1)}), s8[4194304]{0:T(1024)(128)(4,1)S(1)}, s32[]{:S(2)}) async-start(s8[4915200]{0:T(1024)(128)(4,1)} %bitcast.32), calls=%async_computation | async-start | bytes 8388608 | tf_op jit(solution)/shard_map/while
  271.9 15.4 %slice-start = ((s8[4915200]{0:T(1024)(128)(4,1)}), s8[4194304]{0:T(1024)(128)(4,1)S(1)}, s32[]{:S(2)}) async-start(s8[4915200]{0:T(1024)(128)(4,1)} %bitcast.32), calls=%async_computation | async-start | bytes 8388608 | tf_op jit(solution)/shard_map/while
  307.2 12.1 %collective-permute-start = (f32[64,86,11]{1,0,2:T(8,128)S(1)}, f32[64,86,11]{1,0,2:T(8,128)S(1)}, u32[]{:S(2)}, u32[]{:S(2)}) collective-permute-start(f32[64,86,11]{1,0,2:T(8,128)S(1)} %slice.118), channel_id=1, source_target_pairs={{0,32},{32,64},{64,96},{96,128},{128,160},{160,192},{192,224},{1,3... | collective-permute-start | bytes 726536 | tf_op jit(solution)/shard_map/ppermute | solution.py:12
  320.5 10.3 %collective-permute-start.1 = (f32[64,86,11]{1,0,2:T(8,128)S(1)}, f32[64,86,11]{1,0,2:T(8,128)S(1)}, u32[]{:S(2)}, u32[]{:S(2)}) collective-permute-start(f32[64,86,11]{1,0,2:T(8,128)S(1)} %get-tuple-element.203), channel_id=1, source_target_pairs={{32,0},{64,32},{96,64},{128,96},{160,128},{192,160},{224,192},{33,... | collective-permute-start | bytes 726536 | tf_op jit(solution)/shard_map/ppermute | solution.py:12
  339.3 19.2 %collective-permute-start.2 = (f32[64,11,128]{2,0,1:T(8,128)S(1)}, f32[64,11,128]{2,0,1:T(8,128)S(1)}, u32[]{:S(2)}, u32[]{:S(2)}) collective-permute-start(f32[64,11,128]{2,0,1:T(8,128)S(1)} %copy.13), channel_id=1, source_target_pairs={{0,1},{1,2},{2,3},{3,4},{4,5},{5,6},{6,7},{7,8},{8,9},{9,10},{10,1... | collective-permute-start | bytes 1081352 | tf_op jit(solution)/shard_map/ppermute | solution.py:12
  356.6 33.6 %collective-permute-start.3 = (f32[64,11,128]{2,0,1:T(8,128)S(1)}, f32[64,11,128]{2,0,1:T(8,128)S(1)}, u32[]{:S(2)}, u32[]{:S(2)}) collective-permute-start(f32[64,11,128]{2,0,1:T(8,128)S(1)} %copy.15), channel_id=1, source_target_pairs={{1,0},{2,1},{3,2},{4,3},{5,4},{6,5},{7,6},{8,7},{9,8},{10,9},{11,1... | collective-permute-start | bytes 1081352 | tf_op jit(solution)/shard_map/ppermute | solution.py:12
  (14 other events, 49.2 us)
where the time goes:
time: 443 us; the launch traced here: 437 us
  matrix products  257 us (58%)
  local copies, waits for them, and re-layouts  111 us (25%)
  other arithmetic  28 us (6%)
  starting transfers between devices  16.2 us (4%)
  waiting for transfers between devices  13.6 us (3%)
  loops' own time  9.61 us (2%)
    dot_general x11, matrix products, spread_class(): jnp.einsum('zyX,yY->zYX', along_x, band(radius, cells_y, wide_y, margin),...  111 us
    dot_general x11, matrix products, spread_class(): jnp.einsum('zYX,zw->wYX', along_y, band(radius, cells_z, cells_z, 0), pre...  88.1 us
    dot_general x11, matrix products, spread_class(): jnp.einsum('zyx,xX->zyX', masked, band(radius, cells_x, wide_x, margin),...  58 us
    scatter-add x3, local copies, waits for them, and re-layouts, per_device(): result.at[:, :margin, :].add(below).at[:, cells_y - margin:, :].add(above)  56.2 us
    while x66, local copies, waits for them, and re-layouts  24.3 us
    ppermute x4, starting transfers between devices, from_behind(): return lax.ppermute(shard, axis, pairs)  16.2 us
    ppermute x4, waiting for transfers between devices, from_behind(): return lax.ppermute(shard, axis, pairs)  13.6 us
    add x2, other arithmetic, per_device(): result.at[:, :margin, :].add(below).at[:, cells_y - margin:, :].add(above)  13.5 us
  transfers between devices with their start and end apart: 4, of which 2 were waited for; matrix products, arithmetic and copies ran while one was open for 10% of the time, Pallas kernels for 0%

commit v1 on v0

v1 whole, which is shorter than its diff:
```python
import functools

import jax
import jax.numpy as jnp
import numpy as np
from jax import lax
from jax.experimental import pallas as pl
from jax.experimental.pallas import tpu as pltpu
from jax.sharding import PartitionSpec as P

RMAX = 12
MARGIN = RMAX - 1
CLASS_GROUPS = ((12, 11), (10, 9), (8, 7), (6, 5), (4, 3), (2,))
Z, CY, CX = 64, 64, 128
HALF = CY // 2
ROWS_X = 160
STEPS = 4
VMEM_LIMIT = 60 * 1024 * 1024


def tent(radius, distance):
    return np.maximum(0, radius - np.abs(distance)).astype(np.float32)


def band_tables():
    z = np.arange(Z)
    rows_z = np.zeros((len(CLASS_GROUPS), 2 * Z, 4 * Z), np.float32)
    for group, classes in enumerate(CLASS_GROUPS):
        for place, radius in enumerate(classes):
            band = tent(radius, z[:, None] - z[None, :])
            rows = slice(place * Z, place * Z + Z)
            rows_z[group, rows, 2 * place * Z : (2 * place + 1) * Z] = band
            rows_z[group, rows, (2 * place + 1) * Z : (2 * place + 2) * Z] = band
    source_x = np.arange(CX)
    outside = np.full(5, 4 * CX)
    target_x = np.concatenate(
        [np.arange(CX), np.arange(-MARGIN, 0), outside, np.arange(CX, CX + MARGIN), outside]
    )
    rows_x = np.zeros((RMAX - 1, ROWS_X, 2 * CX), np.float32)
    for radius in range(2, RMAX + 1):
        band = tent(radius, target_x[:, None] - source_x[None, :])
        rows_x[radius - 2] = np.concatenate([band, band], axis=1)
    return rows_z.astype(jnp.bfloat16), rows_x.astype(jnp.bfloat16)


def split(value):
    high = value.astype(jnp.bfloat16)
    low = (value - high.astype(jnp.float32)).astype(jnp.bfloat16)
    return high, low


def span(reach, edge):
    short = jnp.maximum(0.0, reach - edge)
    return reach * reach - 0.5 * (short * short + short)


def smear_kernel(
    place_ref, class_ref, sharp_ref, thresh_ref,
    fil0, fil1, ups0, ups1, rad0, rad1, band_z, band_x,
    main_ref, left_ref, right_ref, up_ref, down_ref,
    high_s, low_s, reach_s, smooth_s, ext_s,
):
    step = pl.program_id(0)
    col, row = place_ref[0], place_ref[1]
    beta, eta = sharp_ref[0], thresh_ref[0]
    one = jnp.ones((8, CX), jnp.float32)
    scale = (beta * one) / (jnp.tanh(beta * eta * one) + jnp.tanh(beta * (1.0 - eta) * one))
    cap = class_ref[0, 0]
    lane = lax.broadcasted_iota(jnp.int32, (8, CX), 1)
    sub = lax.broadcasted_iota(jnp.int32, (8, CX), 0)
    far = jnp.full((8, CX), 4096, jnp.int32)
    edge_x = jnp.minimum(
        jnp.where(col == 0, lane, far), jnp.where(col == pl.num_programs(0) * 2 - 1, CX - 1 - lane, far)
    )
    edge_x = (edge_x + 1).astype(jnp.float32)

    def sources(half, fil, ups, rad):
        def one_row(y, _):
            y_in = (step + half * STEPS) * 8 + y
            edge_y = jnp.minimum(
                jnp.where(row == 0, y_in, 4096), jnp.where(row == 31, CY - 1 - y_in, 4096)
            )
            edge_y = (edge_y + 1).astype(jnp.float32)
            for zt in range(Z // 16):
                parts = []
                for zg in (2 * zt, 2 * zt + 1):
                    at = (pl.ds(zg * 64 + y, 8, stride=8), slice(None))
                    reach = jnp.minimum(rad[at], cap).astype(jnp.float32)
                    bend = jnp.tanh(beta * (fil[at] - eta))
                    slope = ups[at] * scale * (1.0 - bend * bend)
                    weight = span(reach, edge_x) * span(reach, edge_y)
                    if zg in (0, 1, 6, 7):
                        z_in = zg * 8 + sub
                        edge_z = (jnp.minimum(z_in, Z - 1 - z_in) + 1).astype(jnp.float32)
                        weight = weight * span(reach, edge_z)
                    else:
                        weight = weight * (reach * reach)
                    parts.append((slope / weight, reach))
                source = jnp.concatenate([parts[0][0], parts[1][0]], axis=0)
                reach = jnp.concatenate([parts[0][1], parts[1][1]], axis=0)
                high, low = split(source)
                at = (half, y, slice(zt * 16, zt * 16 + 16))
                high_s[at] = high
                low_s[at] = low
                reach_s[at] = reach.astype(jnp.bfloat16)
            return 0

        lax.fori_loop(0, 8, one_row, 0)

    sources(0, fil0, ups0, rad0)
    sources(1, fil1, ups1, rad1)

    def quad(pair, _):
        lines = []
        for j in (2 * pair, 2 * pair + 1):
            wide = lambda ref: jnp.concatenate([ref[0, j], ref[1, j]], axis=1)
            lines.append((wide(high_s), wide(low_s), wide(reach_s)))
        for group, classes in enumerate(CLASS_GROUPS):
            depth = 2 * Z * len(classes)
            held = []
            for high, low, reach in lines:
                pieces = []
                for radius in classes:
                    same = reach == jnp.bfloat16(radius)
                    pieces.append(jnp.where(same, high, jnp.bfloat16(0)))
                    pieces.append(jnp.where(same, low, jnp.bfloat16(0)))
                held.append(
                    jnp.dot(
                        band_z[group, : Z * len(classes), :depth],
                        jnp.concatenate(pieces, axis=0),
                        preferred_element_type=jnp.float32,
                    )
                )
            for place, radius in enumerate(classes):
                stack = []
                for part in held:
                    high, low = split(part[place * Z : place * Z + Z])
                    for side in (slice(0, CX), slice(CX, 2 * CX)):
                        stack.append(jnp.concatenate([high[:, side], low[:, side]], axis=1))
                moved = lax.dot_general(
                    band_x[radius - 2],
                    jnp.concatenate(stack, axis=0),
                    (((1,), (1,)), ((), ())),
                    preferred_element_type=jnp.float32,
                )
                t = step * 8 + pair * 2
                smooth_s[radius - 2, t] = moved[:, :CX]
                smooth_s[radius - 2, t + 1] = moved[:, CX:]
        return 0

    lax.fori_loop(0, 4, quad, 0)

    @pl.when(step == STEPS - 1)
    def _():
        def tile(k, _):
            rows = pl.ds(pl.multiple_of(k * 8, 8), 8)
            total = {}
            for t in range(HALF):
                grown = smooth_s[RMAX - 2, t, rows]
                suffix = grown
                for d in range(MARGIN, -1, -1):
                    if d < MARGIN:
                        if d + 1 >= 2:
                            suffix = suffix + smooth_s[d - 1, t, rows]
                        grown = grown + suffix
                    for target in {t + d, t - d}:
                        total[target] = total[target] + grown if target in total else grown
                ext_s[t - MARGIN + MARGIN, rows] = total.pop(t - MARGIN)
            for target in sorted(total):
                ext_s[target + MARGIN, rows] = total[target]
            return 0

        lax.fori_loop(0, ROWS_X // 8, tile, 0)
        upper = lax.broadcasted_iota(jnp.int32, (ROWS_X, CX), 1) >= Z

        def packed(keep, over):
            first = jnp.concatenate([over[:64], over[128:136], over[144:152]], axis=0)
            second = jnp.concatenate([over[64:128], over[136:144], over[152:160]], axis=0)
            return jnp.where(keep[:80], first, pltpu.roll(second, Z, 1))

        for t in range(HALF):
            full = ext_s[t + MARGIN]
            if t < MARGIN:
                over = ext_s[t + HALF + MARGIN]
                full = full + jnp.where(upper, pltpu.roll(over, Z, 1), 0.0)
                up_ref[t] = packed(upper, over)
            if t >= HALF - MARGIN:
                over = ext_s[t - HALF + MARGIN]
                full = full + jnp.where(upper, 0.0, pltpu.roll(over, Z, 1))
                down_ref[t - (HALF - MARGIN)] = packed(~upper, over)
            main_ref[t] = full[:CX]
            left_ref[t] = full[128:144]
            right_ref[t] = full[144:160]


def smear(place, brick_class, sharpness, threshold, filtered, upstream, radius_map, band_z, band_x):
    smem = pl.BlockSpec(memory_space=pltpu.SMEM)
    flat = [a for a in (filtered, upstream, radius_map)]
    block = [
        pl.BlockSpec((Z, 8, CX), functools.partial(lambda h, i: (0, i + h * STEPS, 0), h)) for h in (0, 1)
    ]
    whole = lambda shape: pl.BlockSpec(shape, lambda i: (0,) * len(shape))
    shapes = [(HALF, CX, CX), (HALF, 16, CX), (HALF, 16, CX), (MARGIN, 80, CX), (MARGIN, 80, CX)]
    return pl.pallas_call(
        smear_kernel_flat,
        grid=(STEPS,),
        out_shape=[jax.ShapeDtypeStruct(s, jnp.float32) for s in shapes],
        in_specs=[smem] * 4
        + [block[0], block[1]] * 3
        + [whole(band_z.shape), whole(band_x.shape)],
        out_specs=[whole(s) for s in shapes],
        scratch_shapes=[
            pltpu.VMEM((2, 8, Z, CX), jnp.bfloat16),
            pltpu.VMEM((2, 8, Z, CX), jnp.bfloat16),
            pltpu.VMEM((2, 8, Z, CX), jnp.bfloat16),
            pltpu.VMEM((RMAX - 1, HALF, ROWS_X, CX), jnp.float32),
            pltpu.VMEM((HALF + 2 * MARGIN, ROWS_X, CX), jnp.float32),
        ],
        compiler_params=pltpu.CompilerParams(vmem_limit_bytes=VMEM_LIMIT),
    )(place, brick_class, sharpness, threshold, *[a for a in flat for _ in (0, 1)], band_z, band_x)


def smear_kernel_flat(*refs):
    refs = list(refs)
    for i in range(4, 10):
        refs[i] = refs[i].reshape(Z * 8, CX)
    smear_kernel(*refs)


def corner_kernel(left, right, from_low, from_high, left_out, right_out):
    upper = lax.broadcasted_iota(jnp.int32, (8, CX), 1) >= Z
    for side, (ref, out) in enumerate(((left, left_out), (right, right_out))):
        rows = slice(64 + 8 * side, 72 + 8 * side)
        for t in range(HALF):
            value = ref[t]
            if t < MARGIN:
                got = from_low[t, rows]
                value = value + jnp.concatenate(
                    [jnp.where(upper, 0.0, pltpu.roll(got, Z, 1)), jnp.where(upper, 0.0, got)], axis=0
                )
            if t >= HALF - MARGIN:
                got = from_high[t - (HALF - MARGIN), rows]
                value = value + jnp.concatenate(
                    [jnp.where(upper, pltpu.roll(got, Z, 1), 0.0), jnp.where(upper, got, 0.0)], axis=0
                )
            out[pl.ds(MARGIN * t, MARGIN)] = value[:MARGIN]


def add_corners(left, right, from_low, from_high):
    return pl.pallas_call(
        corner_kernel,
        out_shape=[jax.ShapeDtypeStruct((HALF * MARGIN, CX), jnp.float32)] * 2,
        compiler_params=pltpu.CompilerParams(vmem_limit_bytes=VMEM_LIMIT),
    )(left, right, from_low, from_high)


def merge_kernel(main, from_low, from_high, from_left, from_right, out, block_s, out_s, sem):
    step = pl.program_id(0)
    upper = lax.broadcasted_iota(jnp.int32, (64, CX), 1) >= Z
    flat = out_s.reshape(Z * CY, CX)

    def copies(i):
        return [
            pltpu.make_async_copy(
                out_s.at[:, pl.ds(h * HALF + i * 8, 8)], out.at[:, pl.ds(h * HALF + i * 8, 8)], sem.at[i, h]
            )
            for h in (0, 1)
        ]

    for i in range(STEPS):

        @pl.when(step == i)
        def _():
            for k in range(8):
                t = i * 8 + k
                value = main[k]
                if t < MARGIN:
                    got = from_low[t, :64]
                    value = value + jnp.concatenate(
                        [jnp.where(upper, 0.0, pltpu.roll(got, Z, 1)), jnp.where(upper, 0.0, got)], axis=0
                    )
                if t >= HALF - MARGIN:
                    got = from_high[t - (HALF - MARGIN), :64]
                    value = value + jnp.concatenate(
                        [jnp.where(upper, pltpu.roll(got, Z, 1), 0.0), jnp.where(upper, got, 0.0)], axis=0
                    )
                block_s[k] = value
                block_s[k, :MARGIN] += from_left[pl.ds(MARGIN * t, MARGIN)]
                block_s[k, CX - MARGIN :] += from_right[pl.ds(MARGIN * t, MARGIN)]
                turned = block_s[k].T
                for h in (0, 1):
                    for zg in range(8):
                        flat[pl.ds(zg * 8 * CY + h * HALF + t, 8, stride=CY), :] = turned[
                            h * Z + zg * 8 : h * Z + zg * 8 + 8
                        ]
            for copy in copies(i):
                copy.start()

    @pl.when(step == STEPS - 1)
    def _():
        for i in range(STEPS):
            for copy in copies(i):
                copy.wait()


def merge(main, from_low, from_high, from_left, from_right):
    whole = lambda shape: pl.BlockSpec(shape, lambda i: (0,) * len(shape))
    halos = (from_low, from_high, from_left, from_right)
    return pl.pallas_call(
        merge_kernel,
        grid=(STEPS,),
        out_shape=jax.ShapeDtypeStruct((Z, CY, CX), jnp.float32),
        in_specs=[pl.BlockSpec((8, CX, CX), lambda i: (i, 0, 0))] + [whole(a.shape) for a in halos],
        out_specs=pl.BlockSpec(memory_space=pl.ANY),
        scratch_shapes=[
            pltpu.VMEM((8, CX, CX), jnp.float32),
            pltpu.VMEM((Z, CY, CX), jnp.float32),
            pltpu.SemaphoreType.DMA((STEPS, 2)),
        ],
        compiler_params=pltpu.CompilerParams(vmem_limit_bytes=VMEM_LIMIT),
    )(main, *halos)


def shifted(value, axis, by):
    length = lax.axis_size(axis)
    return lax.ppermute(value, axis, [(i, i + by) for i in range(length) if 0 <= i + by < length])


def per_device(filtered, upstream, radius_map, brick_class, sharpness, threshold):
    rows_z, rows_x = band_tables()
    place = jnp.stack([lax.axis_index("gx"), lax.axis_index("gy")]).astype(jnp.int32)
    main, left, right, up, down = smear(
        place, brick_class, sharpness, threshold, filtered, upstream, radius_map,
        jnp.asarray(rows_z), jnp.asarray(rows_x),
    )
    from_low = shifted(up, "gy", 1)
    from_high = shifted(down, "gy", -1)
    left, right = add_corners(left, right, from_low, from_high)
    from_left = shifted(right, "gx", 1)
    from_right = shifted(left, "gx", -1)
    return merge(main, from_low, from_high, from_left, from_right)


def solution(mesh):
    return jax.shard_map(
        per_device,
        mesh=mesh,
        in_specs=(
            P(None, "gy", "gx"),
            P(None, "gy", "gx"),
            P(None, "gy", "gx"),
            P("gx", "gy"),
            P(),
            P(),
        ),
        out_specs=P(None, "gy", "gx"),
        check_vma=False,
    )
```

time: 443 us -> 85.6 us (0.19); the launches traced: 437 us -> 84.5 us
  matrix products: 257 us -> 0 us
  local copies, waits for them, and re-layouts: 111 us -> 1.46 us
  Pallas kernels: 0 us -> 45.9 us
  other arithmetic: 28 us -> 0.64 us
  loops' own time: 9.61 us -> 0 us
  waiting for transfers between devices: 13.6 us -> 20.1 us
    dot_general x33 -> x0, matrix products: 257 us -> none  [the longest x11 111 us: spread_class(): jnp.einsum('zyX,yY->zYX', along_x, band(radius, cells_y, wide_y, margin),...]
    scatter-add x3 -> x0, local copies, waits for them, and re-layouts: 56.2 us -> none  [per_device(): result.at[:, :margin, :].add(below).at[:, cells_y - margin:, :].add(above)]
    pallas_call x0 -> x3, Pallas kernels: none -> 45.9 us  [the longest x1 38.6 us: smear(): pl.pallas_call(smear_kernel_flat, grid=(STEPS,), out_shape=[jax.ShapeDtyp...]
    while x66 -> x0, local copies, waits for them, and re-layouts: 24.3 us -> none
    slice x6 -> x0, local copies, waits for them, and re-layouts: 21.1 us -> none  [the longest x2 8.47 us: per_device(): above = from_behind(interior[:, :margin, :], 'gy', -1)]
    add x4 -> x0, other arithmetic: 13.5 us -> none  [the longest x2 13.5 us: per_device(): result.at[:, :margin, :].add(below).at[:, cells_y - margin:, :].add(above)]
    div x1 -> x0, other arithmetic: 13.1 us -> none  [per_device(): source = slope / weight_sum]
    another operation x1 -> x0, loops' own time: 9.61 us -> none  [per_device(): lax.fori_loop(2, upper_class, spread_class, jnp.zeros((cells_z, wide_y, w...]
  transfers between devices with their start and end apart: 4 -> 4, of which waited for: 2 -> 4; matrix products, arithmetic and copies ran while one was open for 10% -> 0% of each run, Pallas kernels for 0% -> 0%
where the time goes in v1:
time: 85.6 us; the launch traced here: 84.5 us
  Pallas kernels  45.9 us (54%)
  waiting for transfers between devices  20.1 us (23%)
  starting transfers between devices  14.4 us (17%)
  between operations  1.98 us (2%)
  local copies, waits for them, and re-layouts  1.46 us (2%)
    pallas_call x1, Pallas kernels, smear(): pl.pallas_call(smear_kernel_flat, grid=(STEPS,), out_shape=[jax.ShapeDtyp...  38.6 us
    ppermute x4, waiting for transfers between devices, shifted(): lax.ppermute(value, axis, [(i, i + by) for i in range(length) if 0 <= i +...  20.1 us
    ppermute x4, starting transfers between devices, shifted(): lax.ppermute(value, axis, [(i, i + by) for i in range(length) if 0 <= i +...  14.4 us
    pallas_call x1, Pallas kernels, merge(): pl.pallas_call(merge_kernel, grid=(STEPS,), out_shape=jax.ShapeDtypeStruc...  5.19 us
    pallas_call x1, Pallas kernels, add_corners(): pl.pallas_call(corner_kernel, out_shape=[jax.ShapeDtypeStruct((HALF * MAR...  2.13 us
  transfers between devices with their start and end apart: 4, of which 4 were waited for; matrix products, arithmetic and copies ran while one was open for 0% of the time, Pallas kernels for 0%

profile of v1, /device:TPU:91, one launch (start us, length us, event | category | flops | bytes accessed | tf_op | source)
XLA Modules:
  0.0 84.5 jit_solution(11504409841873596516)
XLA Ops:
  1.9 0.6 pad_add_fusion.refs_0_
  2.6 38.6 %shard_map.82 = (f32[32,128,128]{2,1,0:T(8,128)}, f32[32,16,128]{2,1,0:T(8,128)}, f32[32,16,128]{2,1,0:T(8,128)}, f32[11,80,128]{2,1,0:T(8,128)}, f32[11,80,128]{2,1,0:T(8,128)}) custom-call(s32[2]{0:T(128)} %pad_add_fusion.refs_0_, s32[1,1]{1,0:T(1,128)S(6)} %copy.9.refs_1_, f32[1]{0:T(128)S(6)} %copy.10.refs_2_, f32[1]{0:T(128)S(6)} %copy.11.refs_3_, ...), custom_call_target="tpu_custom_call" | custom-call | tf_op jit(solution)/shard_map/pallas_call | solution.py:204
  41.2 6.3 %collective-permute-start = (f32[11,80,128]{2,1,0:T(8,128)}, f32[11,80,128]{2,1,0:T(8,128)S(1)}, u32[]{:S(2)}, u32[]{:S(2)}) collective-permute-start(f32[11,80,128]{2,1,0:T(8,128)} %get-tuple-element.13), channel_id=1, source_target_pairs={{0,1},{1,2},{2,3},{3,4},{4,5},{5,6},{6,7},{7,8},{8,9},{9,10},{10,1... | collective-permute-start | bytes 1351688 | tf_op jit(solution)/shard_map/ppermute | solution.py:326
  47.5 1.9 %collective-permute-start.1 = (f32[11,80,128]{2,1,0:T(8,128)}, f32[11,80,128]{2,1,0:T(8,128)S(1)}, u32[]{:S(2)}, u32[]{:S(2)}) collective-permute-start(f32[11,80,128]{2,1,0:T(8,128)} %get-tuple-element.14), channel_id=1, source_target_pairs={{1,0},{2,1},{3,2},{4,3},{5,4},{6,5},{7,6},{8,7},{9,8},{10,9},{11,1... | collective-permute-start | bytes 1351688 | tf_op jit(solution)/shard_map/ppermute | solution.py:326
  49.4 8.5 %collective-permute-done.from_low = f32[11,80,128]{2,1,0:T(8,128)S(1)} collective-permute-done((f32[11,80,128]{2,1,0:T(8,128)}, f32[11,80,128]{2,1,0:T(8,128)S(1)}, u32[]{:S(2)}, u32[]{:S(2)}) %collective-permute-start) | collective-permute-done | bytes 450592 | tf_op jit(solution)/shard_map/ppermute | solution.py:326
  57.9 0.0 copy-start
  57.9 8.6 %collective-permute-done.1.from_high = f32[11,80,128]{2,1,0:T(8,128)S(1)} collective-permute-done((f32[11,80,128]{2,1,0:T(8,128)}, f32[11,80,128]{2,1,0:T(8,128)S(1)}, u32[]{:S(2)}, u32[]{:S(2)}) %collective-permute-start.1) | collective-permute-done | bytes 450592 | tf_op jit(solution)/shard_map/ppermute | solution.py:326
  66.5 0.0 copy-start.1
  66.5 0.0 copy-done
  66.5 0.8 copy-done.1
  67.3 2.1 %shard_map.83 = (f32[352,128]{1,0:T(8,128)}, f32[352,128]{1,0:T(8,128)}) custom-call(f32[32,16,128]{2,1,0:T(8,128)} %get-tuple-element.15.left, f32[32,16,128]{2,1,0:T(8,128)} %get-tuple-element.16.right, f32[11,80,128]{2,1,0:T(8,128)} %copy-done, f32[11,80,128]{2,1,0:T(8,128)} %copy-done.1), custom_call_target="tpu_custom_call" | custom-call | tf_op jit(solution)/shard_map/pallas_call | solution.py:250
  69.4 2.2 %collective-permute-start.2 = (f32[352,128]{1,0:T(8,128)}, f32[352,128]{1,0:T(8,128)S(1)}, u32[]{:S(2)}, u32[]{:S(2)}) collective-permute-start(f32[352,128]{1,0:T(8,128)} %get-tuple-element.17), channel_id=1, source_target_pairs={{0,32},{32,64},{64,96},{96,128},{128,160},{160,192},{192,224},{1,3... | collective-permute-start | bytes 540680 | tf_op jit(solution)/shard_map/ppermute | solution.py:326
  71.6 4.0 %collective-permute-start.3 = (f32[352,128]{1,0:T(8,128)}, f32[352,128]{1,0:T(8,128)S(1)}, u32[]{:S(2)}, u32[]{:S(2)}) collective-permute-start(f32[352,128]{1,0:T(8,128)} %get-tuple-element.18), channel_id=1, source_target_pairs={{32,0},{64,32},{96,64},{128,96},{160,128},{192,160},{224,192},{33,... | collective-permute-start | bytes 540680 | tf_op jit(solution)/shard_map/ppermute | solution.py:326
  75.6 1.2 %collective-permute-done.2.from_left = f32[352,128]{1,0:T(8,128)S(1)} collective-permute-done((f32[352,128]{1,0:T(8,128)}, f32[352,128]{1,0:T(8,128)S(1)}, u32[]{:S(2)}, u32[]{:S(2)}) %collective-permute-start.2) | collective-permute-done | bytes 180256 | tf_op jit(solution)/shard_map/ppermute | solution.py:326
  76.8 0.0 copy-start.2
  76.8 1.9 %collective-permute-done.3.from_right = f32[352,128]{1,0:T(8,128)S(1)} collective-permute-done((f32[352,128]{1,0:T(8,128)}, f32[352,128]{1,0:T(8,128)S(1)}, u32[]{:S(2)}, u32[]{:S(2)}) %collective-permute-start.3) | collective-permute-done | bytes 180256 | tf_op jit(solution)/shard_map/ppermute | solution.py:326
  78.6 0.0 copy-start.3
  78.6 0.0 copy-done.2
  78.6 0.7 copy-done.3
  79.3 5.2 %shard_map.84 = f32[64,64,128]{2,1,0:T(8,128)} custom-call(f32[32,128,128]{2,1,0:T(8,128)} %get-tuple-element.12.main, f32[11,80,128]{2,1,0:T(8,128)} %copy-done, f32[11,80,128]{2,1,0:T(8,128)} %copy-done.1, f32[352,128]{1,0:T(8,128)} %copy-done.2, f32[352,128]{1,0:T(8,128)} %copy-done.3), custom_call_target="tpu_custom_call" | custom-call | tf_op jit(solution)/shard_map/pallas_call | solution.py:309
Async XLA Ops:
  41.2 16.7 %collective-permute-start = (f32[11,80,128]{2,1,0:T(8,128)}, f32[11,80,128]{2,1,0:T(8,128)S(1)}, u32[]{:S(2)}, u32[]{:S(2)}) collective-permute-start(f32[11,80,128]{2,1,0:T(8,128)} %get-tuple-element.13), channel_id=1, source_target_pairs={{0,1},{1,2},{2,3},{3,4},{4,5},{5,6},{6,7},{7,8},{8,9},{9,10},{10,1... | collective-permute-start | bytes 1351688 | tf_op jit(solution)/shard_map/ppermute | solution.py:326
  47.5 19.0 %collective-permute-start.1 = (f32[11,80,128]{2,1,0:T(8,128)}, f32[11,80,128]{2,1,0:T(8,128)S(1)}, u32[]{:S(2)}, u32[]{:S(2)}) collective-permute-start(f32[11,80,128]{2,1,0:T(8,128)} %get-tuple-element.14), channel_id=1, source_target_pairs={{1,0},{2,1},{3,2},{4,3},{5,4},{6,5},{7,6},{8,7},{9,8},{10,9},{11,1... | collective-permute-start | bytes 1351688 | tf_op jit(solution)/shard_map/ppermute | solution.py:326
  57.9 8.6 %copy-start = (f32[11,80,128]{2,1,0:T(8,128)}, f32[11,80,128]{2,1,0:T(8,128)S(1)}, u32[]{:S(2)}) copy-start(f32[11,80,128]{2,1,0:T(8,128)S(1)} %collective-permute-done.from_low) | copy-start | bytes 1351684
  66.5 0.8 copy-start.1
  69.4 7.3 %collective-permute-start.2 = (f32[352,128]{1,0:T(8,128)}, f32[352,128]{1,0:T(8,128)S(1)}, u32[]{:S(2)}, u32[]{:S(2)}) collective-permute-start(f32[352,128]{1,0:T(8,128)} %get-tuple-element.17), channel_id=1, source_target_pairs={{0,32},{32,64},{64,96},{96,128},{128,160},{160,192},{192,224},{1,3... | collective-permute-start | bytes 540680 | tf_op jit(solution)/shard_map/ppermute | solution.py:326
  71.6 7.0 %collective-permute-start.3 = (f32[352,128]{1,0:T(8,128)}, f32[352,128]{1,0:T(8,128)S(1)}, u32[]{:S(2)}, u32[]{:S(2)}) collective-permute-start(f32[352,128]{1,0:T(8,128)} %get-tuple-element.18), channel_id=1, source_target_pairs={{32,0},{64,32},{96,64},{128,96},{160,128},{192,160},{224,192},{33,... | collective-permute-start | bytes 540680 | tf_op jit(solution)/shard_map/ppermute | solution.py:326
  76.8 1.9 %copy-start.2 = (f32[352,128]{1,0:T(8,128)}, f32[352,128]{1,0:T(8,128)S(1)}, u32[]{:S(2)}) copy-start(f32[352,128]{1,0:T(8,128)S(1)} %collective-permute-done.2.from_left) | copy-start | bytes 540676
  78.6 0.7 copy-start.3

commit v2 on v1

v2 whole, which is shorter than its diff:
```python
import functools

import jax
import jax.numpy as jnp
import numpy as np
from jax import lax
from jax.experimental import pallas as pl
from jax.experimental.pallas import tpu as pltpu
from jax.sharding import PartitionSpec as P

RMAX = 12
MARGIN = RMAX - 1
Z, CY, CX = 64, 64, 128
HALF = CY // 2
ROWS_X = 160
STEPS = 4
ZROWS = 2
PART = HALF // 2
REACHED = PART + MARGIN
VMEM_LIMIT = 60 * 1024 * 1024


def tent(radius, distance):
    return np.maximum(0, radius - np.abs(distance)).astype(np.float32)


def band_tables():
    z = np.arange(Z)
    outside = np.full(5, 4 * CX)
    source_x = np.arange(CX)
    target_x = np.concatenate(
        [np.arange(CX), np.arange(-MARGIN, 0), outside, np.arange(CX, CX + MARGIN), outside]
    )
    rows_z, rows_x = [], []
    for radius in range(2, RMAX + 1):
        band = np.kron(np.eye(2, dtype=np.float32), tent(radius, z[:, None] - z[None, :]))
        rows_z.append(band)
        rows_x.append(tent(radius, target_x[:, None] - source_x[None, :]))
    return np.stack(rows_z).astype(jnp.bfloat16), np.stack(rows_x).astype(jnp.bfloat16)


def split(value):
    high = value.astype(jnp.bfloat16)
    low = (value - high.astype(jnp.float32)).astype(jnp.bfloat16)
    return high, low


def span(reach, edge):
    short = jnp.maximum(0.0, reach - edge)
    return reach * reach - 0.5 * (short * short + short)


def smear_kernel(part, *refs):
    place_ref, class_ref, sharp_ref, thresh_ref = refs[:4]
    fil, ups, rad = ([ref.reshape(Z * 8, CX) for ref in refs[k : k + 2]] for k in (4, 6, 8))
    band_z, band_x = refs[10:12]
    if part == 0:
        up_ref, down_ref, part_ref = refs[12:15]
    else:
        part_ref, main_ref, left_ref, right_ref = refs[12:16]
    source_s, reach_s, grown_s, smooth_s, ext_s = refs[-5:]
    step = pl.program_id(0)
    col, row = place_ref[0], place_ref[1]
    beta, eta = sharp_ref[0], thresh_ref[0]
    one = jnp.ones((8, CX), jnp.float32)
    scale = (beta * one) / (jnp.tanh(beta * eta * one) + jnp.tanh(beta * (1.0 - eta) * one))
    cap = class_ref[0, 0]
    lane = lax.broadcasted_iota(jnp.int32, (8, CX), 1)
    sub = lax.broadcasted_iota(jnp.int32, (8, CX), 0)
    far = jnp.full((8, CX), 4096, jnp.int32)
    edge_x = jnp.minimum(jnp.where(col == 0, lane, far), jnp.where(col == 7, CX - 1 - lane, far))
    edge_x = (edge_x + 1).astype(jnp.float32)

    def one_row(k, _):
        sides = []
        for half in (0, 1):
            y = k if half == 0 else 7 - k
            from_edge = part * PART + step * 8 + k
            at_edge = row == (0 if half == 0 else 31)
            edge_y = (jnp.where(at_edge, from_edge, 4096) + 1).astype(jnp.float32)
            for zg in range(Z // 8):
                at = (pl.ds(zg * 64 + y, 8, stride=8), slice(None))
                reach = jnp.minimum(rad[half][at], cap).astype(jnp.float32)
                bend = jnp.tanh(beta * (fil[half][at] - eta))
                slope = ups[half][at] * scale * (1.0 - bend * bend)
                weight = span(reach, edge_x) * span(reach, edge_y)
                if zg in (0, 1, 6, 7):
                    z_in = zg * 8 + sub
                    edge_z = (jnp.minimum(z_in, Z - 1 - z_in) + 1).astype(jnp.float32)
                    weight = weight * span(reach, edge_z)
                else:
                    weight = weight * (reach * reach)
                sides.append((slope / weight, reach))
        source = jnp.concatenate([a for a, _ in sides], axis=0).T
        high, low = split(source)
        source_s[k, :, :CX] = high
        source_s[k, :, CX:] = low
        reach_s[k] = jnp.concatenate([b for _, b in sides], axis=0).T.astype(jnp.bfloat16)
        return 0

    lax.fori_loop(0, 8, one_row, 0)

    def along_z(c):
        radius = jnp.bfloat16(c + 2)
        none = jnp.zeros((), jnp.bfloat16)
        both_z = jnp.concatenate([band_z[c], band_z[c]], axis=0)
        for k in range(0, 8, ZROWS):
            pieces = []
            for n in range(k, k + ZROWS):
                same = reach_s[n] == radius
                pieces.append(
                    jnp.concatenate(
                        [jnp.where(same, source_s[n, :, :CX], none), jnp.where(same, source_s[n, :, CX:], none)],
                        axis=1,
                    )
                )
            grown = jnp.dot(jnp.concatenate(pieces, axis=0), both_z, preferred_element_type=jnp.float32)
            high, low = split(grown)
            for n in range(ZROWS):
                rows = slice(n * CX, n * CX + CX)
                line = k + n
                lanes = slice((line % 2) * CX, (line % 2) * CX + CX)
                grown_s[c % 2, line // 2, :CX, lanes] = high[rows]
                grown_s[c % 2, line // 2, CX:, lanes] = low[rows]

    def along_x(c):
        both_x = jnp.concatenate([band_x[c], band_x[c]], axis=1)
        for k in range(4):
            moved = jnp.dot(both_x, grown_s[c % 2, k], preferred_element_type=jnp.float32)
            smooth_s[c, step * 8 + 2 * k] = moved[:, :CX]
            smooth_s[c, step * 8 + 2 * k + 1] = moved[:, CX:]

    along_z(0)
    for c in range(RMAX - 1):
        if c + 1 < RMAX - 1:
            along_z(c + 1)
        along_x(c)

    @pl.when(step == PART // 8 - 1)
    def _():
        first = part * PART - MARGIN

        def keep(t, rows, value):
            if part == 0 and t >= 0:
                part_ref[t, rows] = value
            else:
                ext_s[t - first, rows] = value

        def tile(k, _):
            rows = pl.ds(pl.multiple_of(k * 8, 8), 8)
            total = {}
            if part == 1:
                total = {t: part_ref[t, rows] for t in range(first, REACHED)}
            for t in range(part * PART, part * PART + PART):
                here = t - part * PART
                grown = smooth_s[RMAX - 2, here, rows]
                suffix = grown
                for d in range(MARGIN, -1, -1):
                    if d < MARGIN:
                        if d + 1 >= 2:
                            suffix = suffix + smooth_s[d - 1, here, rows]
                        grown = grown + suffix
                    for target in {t + d, t - d}:
                        total[target] = total[target] + grown if target in total else grown
                keep(t - MARGIN, rows, total.pop(t - MARGIN))
            for target in sorted(total):
                keep(target, rows, total[target])
            return 0

        lax.fori_loop(0, ROWS_X // 8, tile, 0)
        if part == 0:
            upper = lax.broadcasted_iota(jnp.int32, (80, CX), 1) >= Z
            for j in range(MARGIN):
                over = ext_s[j]
                one = jnp.concatenate([over[:64], over[128:136], over[144:152]], axis=0)
                two = jnp.concatenate([over[64:128], over[136:144], over[152:160]], axis=0)
                up_ref[j] = jnp.where(upper, one, pltpu.roll(two, Z, 1))
                down_ref[j] = jnp.where(upper, pltpu.roll(two, Z, 1), one)
        else:
            for t in range(HALF):
                full = part_ref[t] if t < first else ext_s[t - first]
                if t >= HALF - MARGIN:
                    full = full + pltpu.roll(ext_s[2 * HALF - 1 - t - first], Z, 1)
                main_ref[t] = full[:CX]
                left_ref[t] = full[128:144]
                right_ref[t] = full[144:160]


def smear(part, scalars, fields, tables, carried=None):
    block = [
        pl.BlockSpec((Z, 8, CX), lambda i: (0, i + part * 2, 0)),
        pl.BlockSpec((Z, 8, CX), lambda i: (0, 7 - i - part * 2, 0)),
    ]
    whole = lambda shape: pl.BlockSpec(shape, lambda i: (0,) * len(shape))
    partial = (REACHED, ROWS_X, CX)
    if part == 0:
        shapes = [(MARGIN, 80, CX), (MARGIN, 80, CX), partial]
    else:
        shapes = [(HALF, CX, CX), (HALF, 16, CX), (HALF, 16, CX)]
    extra = [] if part == 0 else [carried]
    return pl.pallas_call(
        functools.partial(smear_kernel, part),
        grid=(PART // 8,),
        out_shape=[jax.ShapeDtypeStruct(s, jnp.float32) for s in shapes],
        in_specs=[pl.BlockSpec(memory_space=pltpu.SMEM)] * 4
        + block * 3
        + [whole(a.shape) for a in tables]
        + [whole(a.shape) for a in extra],
        out_specs=[whole(s) for s in shapes],
        scratch_shapes=[
            pltpu.VMEM((8, CX, 2 * CX), jnp.bfloat16),
            pltpu.VMEM((8, CX, CX), jnp.bfloat16),
            pltpu.VMEM((2, 4, 2 * CX, 2 * CX), jnp.bfloat16),
            pltpu.VMEM((RMAX - 1, PART, ROWS_X, CX), jnp.float32),
            pltpu.VMEM((PART + 2 * MARGIN, ROWS_X, CX), jnp.float32),
        ],
        compiler_params=pltpu.CompilerParams(vmem_limit_bytes=VMEM_LIMIT),
        cost_estimate=pl.CostEstimate(flops=8_000_000_000, bytes_accessed=8_000_000, transcendentals=262144),
        name="edge_rows" if part == 0 else "middle_rows",
    )(*scalars, *[a for a in fields for _ in (0, 1)], *tables, *extra)


def arriving(from_low, from_high, rows):
    low, high = from_low[rows], from_high[rows]
    upper = lax.broadcasted_iota(jnp.int32, low.shape, 1) >= Z
    return jnp.concatenate(
        [pltpu.roll(jnp.where(upper, low, high), Z, 1), jnp.where(upper, high, low)], axis=0
    )


def corner_kernel(left, right, from_low, from_high, left_out, right_out):
    for side, (ref, out) in enumerate(((left, left_out), (right, right_out))):
        rows = slice(64 + 8 * side, 72 + 8 * side)
        for t in range(HALF):
            value = ref[t]
            if t < MARGIN:
                j = MARGIN - 1 - t
                value = value + arriving(from_low.at[j], from_high.at[j], rows)
            out[pl.ds(MARGIN * t, MARGIN)] = value[:MARGIN]


def add_corners(left, right, from_low, from_high):
    return pl.pallas_call(
        corner_kernel,
        out_shape=[jax.ShapeDtypeStruct((HALF * MARGIN, CX), jnp.float32)] * 2,
        compiler_params=pltpu.CompilerParams(vmem_limit_bytes=VMEM_LIMIT),
    )(left, right, from_low, from_high)


def merge_kernel(main, from_low, from_high, from_left, from_right, out, block_s, out_s, sem):
    step = pl.program_id(0)
    flat = out_s.reshape(Z * CY, CX)

    def copies(i):
        return [
            pltpu.make_async_copy(
                out_s.at[:, pl.ds(y, 8)], out.at[:, pl.ds(y, 8)], sem.at[i, h]
            )
            for h, y in enumerate((i * 8, CY - 8 - i * 8))
        ]

    for i in range(STEPS):

        @pl.when(step == i)
        def _():
            for k in range(8):
                t = i * 8 + k
                value = main[k]
                if t < MARGIN:
                    j = MARGIN - 1 - t
                    value = value + arriving(from_low.at[j], from_high.at[j], slice(0, 64))
                block_s[k] = value
                block_s[k, :MARGIN] += from_left[pl.ds(MARGIN * t, MARGIN)]
                block_s[k, CX - MARGIN :] += from_right[pl.ds(MARGIN * t, MARGIN)]
                turned = block_s[k].T
                for h, y in enumerate((t, CY - 1 - t)):
                    for zg in range(8):
                        flat[pl.ds(zg * 8 * CY + y, 8, stride=CY), :] = turned[
                            h * Z + zg * 8 : h * Z + zg * 8 + 8
                        ]
            for copy in copies(i):
                copy.start()

    @pl.when(step == STEPS - 1)
    def _():
        for i in range(STEPS):
            for copy in copies(i):
                copy.wait()


def merge(main, from_low, from_high, from_left, from_right):
    whole = lambda shape: pl.BlockSpec(shape, lambda i: (0,) * len(shape))
    halos = (from_low, from_high, from_left, from_right)
    return pl.pallas_call(
        merge_kernel,
        grid=(STEPS,),
        out_shape=jax.ShapeDtypeStruct((Z, CY, CX), jnp.float32),
        in_specs=[pl.BlockSpec((8, CX, CX), lambda i: (i, 0, 0))] + [whole(a.shape) for a in halos],
        out_specs=pl.BlockSpec(memory_space=pl.ANY),
        scratch_shapes=[
            pltpu.VMEM((8, CX, CX), jnp.float32),
            pltpu.VMEM((Z, CY, CX), jnp.float32),
            pltpu.SemaphoreType.DMA((STEPS, 2)),
        ],
        compiler_params=pltpu.CompilerParams(vmem_limit_bytes=VMEM_LIMIT),
    )(main, *halos)


def shifted(value, axis, by):
    length = lax.axis_size(axis)
    return lax.ppermute(value, axis, [(i, i + by) for i in range(length) if 0 <= i + by < length])


def per_device(filtered, upstream, radius_map, brick_class, sharpness, threshold):
    rows_z, rows_x = band_tables()
    place = jnp.stack([lax.axis_index("gx"), lax.axis_index("gy")]).astype(jnp.int32)
    scalars = (place, brick_class, sharpness, threshold)
    fields = (filtered, upstream, radius_map)
    tables = (jnp.asarray(rows_z), jnp.asarray(rows_x))
    up, down, carried = smear(0, scalars, fields, tables)
    from_low = shifted(up, "gy", 1)
    from_high = shifted(down, "gy", -1)
    main, left, right = smear(1, scalars, fields, tables, carried)
    left, right = add_corners(left, right, from_low, from_high)
    from_left = shifted(right, "gx", 1)
    from_right = shifted(left, "gx", -1)
    return merge(main, from_low, from_high, from_left, from_right)


def solution(mesh):
    return jax.shard_map(
        per_device,
        mesh=mesh,
        in_specs=(
            P(None, "gy", "gx"),
            P(None, "gy", "gx"),
            P(None, "gy", "gx"),
            P("gx", "gy"),
            P(),
            P(),
        ),
        out_specs=P(None, "gy", "gx"),
        check_vma=False,
    )
```

time: 85.6 us -> 63.4 us (0.74)
  the two profiles are of different devices: /device:TPU:91 before, /device:TPU:162 now
where the time goes in v2:
time: 63.4 us; the launch traced here: 63.1 us
  Pallas kernels  36.8 us (58%)
  starting transfers between devices  15.6 us (25%)
  waiting for transfers between devices  6.49 us (10%)
  between operations  2.01 us (3%)
  local copies, waits for them, and re-layouts  1.59 us (3%)
    pallas_call x2, Pallas kernels, smear(): pl.pallas_call(functools.partial(smear_kernel, part), grid=(PART // 8,),...  29.6 us
    ppermute x4, starting transfers between devices, shifted(): lax.ppermute(value, axis, [(i, i + by) for i in range(length) if 0 <= i +...  15.6 us
    ppermute x4, waiting for transfers between devices, shifted(): lax.ppermute(value, axis, [(i, i + by) for i in range(length) if 0 <= i +...  6.49 us
    pallas_call x1, Pallas kernels, merge(): pl.pallas_call(merge_kernel, grid=(STEPS,), out_shape=jax.ShapeDtypeStruc...  5.1 us
    pallas_call x1, Pallas kernels, add_corners(): pl.pallas_call(corner_kernel, out_shape=[jax.ShapeDtypeStruct((HALF * MAR...  2.12 us
    unnamed x8, local copies, waits for them, and re-layouts  1.59 us
  transfers between devices with their start and end apart: 4, of which 2 were waited for; matrix products, arithmetic and copies ran while one was open for 0% of the time, Pallas kernels for 24%

profile of v2, /device:TPU:162, one launch (start us, length us, event | category | flops | bytes accessed | tf_op | source)
XLA Modules:
  0.0 63.1 jit_solution(11521892650247573793)
XLA Ops:
  1.9 0.6 pad_add_fusion.refs_0_
  2.6 14.3 %edge_rows.1 = (f32[11,80,128]{2,1,0:T(8,128)}, f32[11,80,128]{2,1,0:T(8,128)}, f32[27,160,128]{2,1,0:T(8,128)}) custom-call(s32[2]{0:T(128)} %pad_add_fusion.refs_0_, s32[1,1]{1,0:T(1,128)S(6)} %copy.9.refs_1_, f32[1]{0:T(128)S(6)} %copy.10.refs_2_, f32[1]{0:T(128)S(6)} %copy.11.refs_3_, f32[64,64,128]{2,1,0:T(8,128)} %refs_5_.3, f32[64,64,128]{2,1,0:T(8,128)} %refs_5_.3, ...), custom_call_target="tpu_custom_call" | custom-call | flops 8000000000 | bytes 8000000 | tf_op jit(solution)/shard_map/edge_rows/pallas_call | solution.py:201
  16.8 1.9 %collective-permute-start = (f32[11,80,128]{2,1,0:T(8,128)}, f32[11,80,128]{2,1,0:T(8,128)S(1)}, u32[]{:S(2)}, u32[]{:S(2)}) collective-permute-start(f32[11,80,128]{2,1,0:T(8,128)} %get-tuple-element.15), channel_id=1, source_target_pairs={{0,1},{1,2},{2,3},{3,4},{4,5},{5,6},{6,7},{7,8},{8,9},{9,10},{10,1... | collective-permute-start | bytes 1351688 | tf_op jit(solution)/shard_map/ppermute | solution.py:311
  18.8 7.9 %collective-permute-start.1 = (f32[11,80,128]{2,1,0:T(8,128)}, f32[11,80,128]{2,1,0:T(8,128)S(1)}, u32[]{:S(2)}, u32[]{:S(2)}) collective-permute-start(f32[11,80,128]{2,1,0:T(8,128)} %get-tuple-element.16), channel_id=1, source_target_pairs={{1,0},{2,1},{3,2},{4,3},{5,4},{6,5},{7,6},{8,7},{9,8},{10,9},{11,1... | collective-permute-start | bytes 1351688 | tf_op jit(solution)/shard_map/ppermute | solution.py:311
  26.6 15.3 %middle_rows.1 = (f32[32,128,128]{2,1,0:T(8,128)}, f32[32,16,128]{2,1,0:T(8,128)}, f32[32,16,128]{2,1,0:T(8,128)}) custom-call(s32[2]{0:T(128)} %pad_add_fusion.refs_0_, s32[1,1]{1,0:T(1,128)S(6)} %copy.9.refs_1_, f32[1]{0:T(128)S(6)} %copy.10.refs_2_, f32[1]{0:T(128)S(6)} %copy.11.refs_3_, f32[64,64,128]{2,1,0:T(8,128)} %refs_5_.3, f32[64,64,128]{2,1,0:T(8,128)} %refs_5_.3, ...), custom_call_target="tpu_custom_call" | custom-call | flops 8000000000 | bytes 8000000 | tf_op jit(solution)/shard_map/middle_rows/pallas_call | solution.py:201
  41.9 0.0 collective-permute-done.from_low
  41.9 0.0 copy-start
  41.9 0.0 collective-permute-done.1.from_high
  41.9 0.0 copy-start.1
  41.9 0.7 %copy-done = f32[11,80,128]{2,1,0:T(8,128)} copy-done((f32[11,80,128]{2,1,0:T(8,128)}, f32[11,80,128]{2,1,0:T(8,128)S(1)}, u32[]{:S(2)}) %copy-start) | copy-done | bytes 450584
  42.7 0.2 copy-done.1
  42.8 2.1 %shard_map.82 = (f32[352,128]{1,0:T(8,128)}, f32[352,128]{1,0:T(8,128)}) custom-call(f32[32,16,128]{2,1,0:T(8,128)} %get-tuple-element.17.left, f32[32,16,128]{2,1,0:T(8,128)} %get-tuple-element.18.right, f32[11,80,128]{2,1,0:T(8,128)} %copy-done, f32[11,80,128]{2,1,0:T(8,128)} %copy-done.1), custom_call_target="tpu_custom_call" | custom-call | tf_op jit(solution)/shard_map/pallas_call | solution.py:243
  44.9 3.8 %collective-permute-start.2 = (f32[352,128]{1,0:T(8,128)}, f32[352,128]{1,0:T(8,128)S(1)}, u32[]{:S(2)}, u32[]{:S(2)}) collective-permute-start(f32[352,128]{1,0:T(8,128)} %get-tuple-element.19), channel_id=1, source_target_pairs={{0,32},{32,64},{64,96},{96,128},{128,160},{160,192},{192,224},{1,3... | collective-permute-start | bytes 540680 | tf_op jit(solution)/shard_map/ppermute | solution.py:311
  48.8 2.0 %collective-permute-start.3 = (f32[352,128]{1,0:T(8,128)}, f32[352,128]{1,0:T(8,128)S(1)}, u32[]{:S(2)}, u32[]{:S(2)}) collective-permute-start(f32[352,128]{1,0:T(8,128)} %get-tuple-element.20), channel_id=1, source_target_pairs={{32,0},{64,32},{96,64},{128,96},{160,128},{192,160},{224,192},{33,... | collective-permute-start | bytes 540680 | tf_op jit(solution)/shard_map/ppermute | solution.py:311
  50.8 2.0 %collective-permute-done.2.from_left = f32[352,128]{1,0:T(8,128)S(1)} collective-permute-done((f32[352,128]{1,0:T(8,128)}, f32[352,128]{1,0:T(8,128)S(1)}, u32[]{:S(2)}, u32[]{:S(2)}) %collective-permute-start.2) | collective-permute-done | bytes 180256 | tf_op jit(solution)/shard_map/ppermute | solution.py:311
  52.8 0.0 copy-start.2
  52.8 4.5 %collective-permute-done.3.from_right = f32[352,128]{1,0:T(8,128)S(1)} collective-permute-done((f32[352,128]{1,0:T(8,128)}, f32[352,128]{1,0:T(8,128)S(1)}, u32[]{:S(2)}, u32[]{:S(2)}) %collective-permute-start.3) | collective-permute-done | bytes 180256 | tf_op jit(solution)/shard_map/ppermute | solution.py:311
  57.3 0.0 copy-start.3
  57.3 0.0 copy-done.2
  57.3 0.7 %copy-done.3 = f32[352,128]{1,0:T(8,128)} copy-done((f32[352,128]{1,0:T(8,128)}, f32[352,128]{1,0:T(8,128)S(1)}, u32[]{:S(2)}) %copy-start.3) | copy-done | bytes 180248
  58.0 5.1 %shard_map.83 = f32[64,64,128]{2,1,0:T(8,128)} custom-call(f32[32,128,128]{2,1,0:T(8,128)} %get-tuple-element.14.main, f32[11,80,128]{2,1,0:T(8,128)} %copy-done, f32[11,80,128]{2,1,0:T(8,128)} %copy-done.1, f32[352,128]{1,0:T(8,128)} %copy-done.2, f32[352,128]{1,0:T(8,128)} %copy-done.3), custom_call_target="tpu_custom_call" | custom-call | tf_op jit(solution)/shard_map/pallas_call | solution.py:294
Async XLA Ops:
  16.8 25.1 %collective-permute-start = (f32[11,80,128]{2,1,0:T(8,128)}, f32[11,80,128]{2,1,0:T(8,128)S(1)}, u32[]{:S(2)}, u32[]{:S(2)}) collective-permute-start(f32[11,80,128]{2,1,0:T(8,128)} %get-tuple-element.15), channel_id=1, source_target_pairs={{0,1},{1,2},{2,3},{3,4},{4,5},{5,6},{6,7},{7,8},{8,9},{9,10},{10,1... | collective-permute-start | bytes 1351688 | tf_op jit(solution)/shard_map/ppermute | solution.py:311
  18.8 23.2 %collective-permute-start.1 = (f32[11,80,128]{2,1,0:T(8,128)}, f32[11,80,128]{2,1,0:T(8,128)S(1)}, u32[]{:S(2)}, u32[]{:S(2)}) collective-permute-start(f32[11,80,128]{2,1,0:T(8,128)} %get-tuple-element.16), channel_id=1, source_target_pairs={{1,0},{2,1},{3,2},{4,3},{5,4},{6,5},{7,6},{8,7},{9,8},{10,9},{11,1... | collective-permute-start | bytes 1351688 | tf_op jit(solution)/shard_map/ppermute | solution.py:311
  41.9 0.8 %copy-start = (f32[11,80,128]{2,1,0:T(8,128)}, f32[11,80,128]{2,1,0:T(8,128)S(1)}, u32[]{:S(2)}) copy-start(f32[11,80,128]{2,1,0:T(8,128)S(1)} %collective-permute-done.from_low) | copy-start | bytes 1351684
  41.9 0.9 %copy-start.1 = (f32[11,80,128]{2,1,0:T(8,128)}, f32[11,80,128]{2,1,0:T(8,128)S(1)}, u32[]{:S(2)}) copy-start(f32[11,80,128]{2,1,0:T(8,128)S(1)} %collective-permute-done.1.from_high) | copy-start | bytes 1351684
  44.9 7.8 %collective-permute-start.2 = (f32[352,128]{1,0:T(8,128)}, f32[352,128]{1,0:T(8,128)S(1)}, u32[]{:S(2)}, u32[]{:S(2)}) collective-permute-start(f32[352,128]{1,0:T(8,128)} %get-tuple-element.19), channel_id=1, source_target_pairs={{0,32},{32,64},{64,96},{96,128},{128,160},{160,192},{192,224},{1,3... | collective-permute-start | bytes 540680 | tf_op jit(solution)/shard_map/ppermute | solution.py:311
  48.8 8.5 %collective-permute-start.3 = (f32[352,128]{1,0:T(8,128)}, f32[352,128]{1,0:T(8,128)S(1)}, u32[]{:S(2)}, u32[]{:S(2)}) collective-permute-start(f32[352,128]{1,0:T(8,128)} %get-tuple-element.20), channel_id=1, source_target_pairs={{32,0},{64,32},{96,64},{128,96},{160,128},{192,160},{224,192},{33,... | collective-permute-start | bytes 540680 | tf_op jit(solution)/shard_map/ppermute | solution.py:311
  52.8 4.5 %copy-start.2 = (f32[352,128]{1,0:T(8,128)}, f32[352,128]{1,0:T(8,128)S(1)}, u32[]{:S(2)}) copy-start(f32[352,128]{1,0:T(8,128)S(1)} %collective-permute-done.2.from_left) | copy-start | bytes 540676
  57.3 0.7 %copy-start.3 = (f32[352,128]{1,0:T(8,128)}, f32[352,128]{1,0:T(8,128)S(1)}, u32[]{:S(2)}) copy-start(f32[352,128]{1,0:T(8,128)S(1)} %collective-permute-done.3.from_right) | copy-start | bytes 540676

commit v3 on v0

v3 whole, which is shorter than its diff:
```python
import functools

import jax
import jax.numpy as jnp
import numpy as np
from jax import lax
from jax.experimental import pallas as pl
from jax.experimental.pallas import tpu as pltpu
from jax.sharding import PartitionSpec as P

RMAX = 12
MARGIN = RMAX - 1
CLASSES = RMAX - 1
Z, CY, CX = 64, 64, 128
HALF = CY // 2
GROUP = 8
PART = HALF // 2
REACHED = PART + MARGIN
RIM = 16
HALO_ROWS = 480
MIB = 1024 * 1024


def tent(radius, distance):
    return np.maximum(0, radius - np.abs(distance)).astype(np.float32)


def band_tables():
    z, x = np.arange(Z), np.arange(CX)
    outside = np.full(RIM - MARGIN, 8 * CX)
    rim_from = np.concatenate([np.arange(RIM), np.arange(CX - RIM, CX)])
    rim_to = np.concatenate([np.arange(-MARGIN, 0), outside, np.arange(CX, CX + MARGIN), outside])
    rows_z, rows_x, rows_rim = [], [], []
    for radius in range(2, RMAX + 1):
        rows_z.append(np.kron(np.eye(2, dtype=np.float32), tent(radius, z[:, None] - z[None, :])))
        rows_x.append(tent(radius, x[:, None] - x[None, :]))
        rim = tent(radius, rim_to[:, None] - rim_from[None, :])
        rows_rim.append(np.kron(np.eye(4, dtype=np.float32), rim))
    return [jnp.asarray(np.stack(rows).astype(jnp.bfloat16)) for rows in (rows_z, rows_x, rows_rim)]


def split(value):
    high = value.astype(jnp.bfloat16)
    low = (value - high.astype(jnp.float32)).astype(jnp.bfloat16)
    return high, low


def span(reach, edge):
    short = jnp.maximum(0.0, reach - edge)
    return reach * reach - 0.5 * (short * short + short)


def whole(shape):
    return pl.BlockSpec(shape, lambda i: (0,) * len(shape))


def along_z(c, high_low, reach, band_z):
    radius = jnp.bfloat16(c + 2)
    none = jnp.zeros((), jnp.bfloat16)
    pieces = []
    for pair, level in zip(high_low, reach):
        same = level == radius
        pieces.append(jnp.concatenate([jnp.where(same, piece, none) for piece in pair], axis=1))
    both = jnp.concatenate([band_z[c], band_z[c]], axis=0)
    return split(jnp.dot(jnp.concatenate(pieces, axis=0), both, preferred_element_type=jnp.float32))


def spread_y(load, times, total, keep):
    for t in times:
        grown = load(RMAX, t)
        suffix = grown
        for d in range(MARGIN, -1, -1):
            if d < MARGIN:
                if d + 1 >= 2:
                    suffix = suffix + load(d + 1, t)
                grown = grown + suffix
            for target in {t + d, t - d}:
                total[target] = total[target] + grown if target in total else grown
        keep(t - MARGIN, total.pop(t - MARGIN))
    for target in sorted(total):
        keep(target, total[target])


def rim_kernel(
    class_ref, sharp_ref, thresh_ref, fil0, fil1, ups0, ups1, rad0, rad1, band_z, band_rim,
    source_ref, reach_ref, left_ref, right_ref, pair_a, pair_b, level_a, level_b, grown_s, smooth_s, ext_s,
):
    fil, ups, rad = (
        [ref.reshape(Z * GROUP, CX) for ref in pair] for pair in ((fil0, fil1), (ups0, ups1), (rad0, rad1))
    )
    step = pl.program_id(0)
    col, row = lax.axis_index("gx"), lax.axis_index("gy")
    last_col, last_row = lax.axis_size("gx") - 1, lax.axis_size("gy") - 1
    beta, eta = sharp_ref[0], thresh_ref[0]
    one = jnp.ones((8, CX), jnp.float32)
    scale = (beta * one) / (jnp.tanh(beta * eta * one) + jnp.tanh(beta * (1.0 - eta) * one))
    cap = class_ref[0, 0]
    lane = lax.broadcasted_iota(jnp.int32, (8, CX), 1)
    sub = lax.broadcasted_iota(jnp.int32, (8, CX), 0)
    far = jnp.full((8, CX), 4096, jnp.int32)
    edge_x = jnp.minimum(jnp.where(col == 0, lane, far), jnp.where(col == last_col, CX - 1 - lane, far))
    edge_x = (edge_x + 1).astype(jnp.float32)

    def one_row(k, pair_s, level_s):
        sides = []
        for half in (0, 1):
            y = k if half == 0 else GROUP - 1 - k
            at_edge = row == (0 if half == 0 else last_row)
            edge_y = (jnp.where(at_edge, step * GROUP + k, 4096) + 1).astype(jnp.float32)
            for zg in range(Z // 8):
                at = (pl.ds(zg * 8 * GROUP + y, 8, stride=GROUP), slice(None))
                reach = jnp.minimum(rad[half][at], cap).astype(jnp.float32)
                bend = jnp.tanh(beta * (fil[half][at] - eta))
                slope = ups[half][at] * scale * (1.0 - bend * bend)
                weight = span(reach, edge_x) * span(reach, edge_y)
                if zg in (0, 1, 6, 7):
                    z_in = zg * 8 + sub
                    edge_z = (jnp.minimum(z_in, Z - 1 - z_in) + 1).astype(jnp.float32)
                    weight = weight * span(reach, edge_z)
                else:
                    weight = weight * (reach * reach)
                sides.append((slope / weight, reach))
        high, low = split(jnp.concatenate([a for a, _ in sides], axis=0).T)
        level = jnp.concatenate([b for _, b in sides], axis=0).T.astype(jnp.bfloat16)
        source_ref[k, :, :CX] = high
        source_ref[k, :, CX:] = low
        reach_ref[k] = level
        for n, rows in enumerate((slice(0, RIM), slice(CX - RIM, CX))):
            pair_s[k, n, :, :CX] = high[rows]
            pair_s[k, n, :, CX:] = low[rows]
            level_s[k, n] = level[rows]

    def rim_z(c, pair_s, level_s):
        for k in range(0, GROUP, 4):
            both = [(n, side) for n in range(k, k + 4) for side in (0, 1)]
            pairs = [(pair_s[n, side, :, :CX], pair_s[n, side, :, CX:]) for n, side in both]
            high, low = along_z(c, pairs, [level_s[n, side] for n, side in both], band_z)
            lanes = slice(k // 4 * CX, k // 4 * CX + CX)
            grown_s[c % 2, :CX, lanes] = high
            grown_s[c % 2, CX:, lanes] = low

    def rim_x(c):
        both = jnp.concatenate([band_rim[c], band_rim[c]], axis=1)
        moved = jnp.dot(both, grown_s[c % 2], preferred_element_type=jnp.float32)
        for k in range(GROUP):
            lanes = slice(k // 4 * CX, k // 4 * CX + CX)
            rows = slice(k % 4 * 2 * RIM, k % 4 * 2 * RIM + 2 * RIM)
            smooth_s[c, (step - 1) * GROUP + k] = moved[rows, lanes]

    def classes(pair_s, level_s, beside):
        rim_z(0, pair_s, level_s)
        for c in range(CLASSES):
            if c + 1 < CLASSES:
                rim_z(c + 1, pair_s, level_s)
            beside(c)
            rim_x(c)

    def beside(pair_s, level_s):
        def go(c):
            if c < GROUP:
                one_row(c, pair_s, level_s)

        return go

    groups = HALF // GROUP

    @pl.when(step == 0)
    def _():
        @pl.loop(0, GROUP)
        def _(k):
            one_row(k, pair_a, level_a)

    @pl.when((step % 2 == 1) & (step < groups))
    def _():
        classes(pair_a, level_a, beside(pair_b, level_b))

    @pl.when((step % 2 == 0) & (step > 0) & (step < groups))
    def _():
        classes(pair_b, level_b, beside(pair_a, level_a))

    @pl.when(step == groups)
    def _():
        classes(pair_b, level_b, lambda c: None)

        def tile(k, _):
            rows = pl.ds(pl.multiple_of(k * 8, 8), 8)

            def keep(t, value):
                ext_s[t + MARGIN, rows] = value

            spread_y(lambda radius, t: smooth_s[radius - 2, t, rows], range(HALF), {}, keep)
            return 0

        lax.fori_loop(0, 2 * RIM // 8, tile, 0)
        for t in range(-MARGIN, HALF):
            full = ext_s[t + MARGIN]
            if t >= HALF - MARGIN:
                full = full + pltpu.roll(ext_s[2 * HALF - 1 - t + MARGIN], Z, 1)
            left_ref[pl.ds(MARGIN * (t + MARGIN), MARGIN)] = full[:MARGIN]
            right_ref[pl.ds(MARGIN * (t + MARGIN), MARGIN)] = full[RIM : RIM + MARGIN]
        for ref in (left_ref, right_ref):
            spare = HALO_ROWS - MARGIN * (HALF + MARGIN)
            ref[pl.ds(HALO_ROWS - spare, spare)] = jnp.zeros((spare, CX), jnp.float32)


def rim(scalars, fields, band_z, band_rim):
    groups = HALF // GROUP
    now = lambda i: jnp.minimum(i, groups - 1)
    block = [
        pl.BlockSpec((Z, GROUP, CX), lambda i: (0, now(i), 0)),
        pl.BlockSpec((Z, GROUP, CX), lambda i: (0, 2 * groups - 1 - now(i), 0)),
    ]
    halo = (HALO_ROWS, CX)
    return pl.pallas_call(
        rim_kernel,
        grid=(groups + 1,),
        out_shape=[
            jax.ShapeDtypeStruct((HALF, CX, 2 * CX), jnp.bfloat16),
            jax.ShapeDtypeStruct((HALF, CX, CX), jnp.bfloat16),
            jax.ShapeDtypeStruct(halo, jnp.float32),
            jax.ShapeDtypeStruct(halo, jnp.float32),
        ],
        in_specs=[pl.BlockSpec(memory_space=pltpu.SMEM)] * 3
        + block * 3
        + [whole(band_z.shape), whole(band_rim.shape)],
        out_specs=[
            pl.BlockSpec((GROUP, CX, 2 * CX), lambda i: (now(i), 0, 0)),
            pl.BlockSpec((GROUP, CX, CX), lambda i: (now(i), 0, 0)),
            whole(halo),
            whole(halo),
        ],
        scratch_shapes=[
            pltpu.VMEM((GROUP, 2, RIM, 2 * CX), jnp.bfloat16),
            pltpu.VMEM((GROUP, 2, RIM, 2 * CX), jnp.bfloat16),
            pltpu.VMEM((GROUP, 2, RIM, CX), jnp.bfloat16),
            pltpu.VMEM((GROUP, 2, RIM, CX), jnp.bfloat16),
            pltpu.VMEM((2, 2 * CX, 2 * CX), jnp.bfloat16),
            pltpu.VMEM((CLASSES, HALF, 2 * RIM, CX), jnp.float32),
            pltpu.VMEM((HALF + 2 * MARGIN, 2 * RIM, CX), jnp.float32),
        ],
        compiler_params=pltpu.CompilerParams(vmem_limit_bytes=60 * MIB),
        cost_estimate=pl.CostEstimate(flops=4_000_000_000, bytes_accessed=11_000_000, transcendentals=524288),
        name="source_and_rim",
    )(*scalars, *[a for a in fields for _ in (0, 1)], band_z, band_rim)


def rows_kernel(part, *refs):
    source_ref, reach_ref, band_z, band_x = refs[:4]
    if part == 0:
        halo_ref, part_ref = refs[4:6]
        grown_s, smooth_s = refs[6:]
    else:
        part_ref, from_left, from_right, edge_ref, out_ref = refs[4:9]
        grown_s, smooth_s, ext_s, out_s, sem = refs[9:]
    step = pl.program_id(0)

    def main_z(c):
        for k in range(0, GROUP, 2):
            pairs = [(source_ref[n, :, :CX], source_ref[n, :, CX:]) for n in (k, k + 1)]
            high, low = along_z(c, pairs, [reach_ref[n] for n in (k, k + 1)], band_z)
            for n in (0, 1):
                here = slice(n * CX, n * CX + CX)
                grown_s[c % 2, k // 2, :CX, here] = high[here]
                grown_s[c % 2, k // 2, CX:, here] = low[here]

    def main_x(c):
        both = jnp.concatenate([band_x[c], band_x[c]], axis=1)
        for k in range(GROUP // 2):
            moved = jnp.dot(both, grown_s[c % 2, k], preferred_element_type=jnp.float32)
            smooth_s[c, step * GROUP + 2 * k] = moved[:, :CX]
            smooth_s[c, step * GROUP + 2 * k + 1] = moved[:, CX:]

    main_z(0)
    for c in range(CLASSES):
        if c + 1 < CLASSES:
            main_z(c + 1)
        main_x(c)

    @pl.when(step == PART // GROUP - 1)
    def _():
        start = part * PART

        def tile(k, _):
            rows = pl.ds(pl.multiple_of(k * 8, 8), 8)

            def keep(t, value):
                if part == 1:
                    ext_s[t, rows] = value
                elif t < 0:
                    halo_ref[t + MARGIN, rows] = value
                else:
                    part_ref[t, rows] = value

            total = {t: part_ref[t, rows] for t in range(start - MARGIN, REACHED)} if part == 1 else {}
            load = lambda radius, t: smooth_s[radius - 2, t - start, rows]
            spread_y(load, range(start, start + PART), total, keep)
            return 0

        lax.fori_loop(0, CX // 8, tile, 0)
        if part == 1:
            flat = out_s.reshape(Z * PART * 2, CX)
            for t in range(HALF):
                at = edge_ref.at[t] if t < PART else ext_s.at[t]
                if t < PART:
                    at[...] = part_ref[t] if t < start - MARGIN else ext_s[t]
                elif t >= HALF - MARGIN:
                    at[...] += pltpu.roll(ext_s[2 * HALF - 1 - t], Z, 1)
                halo = pl.ds(MARGIN * (t + MARGIN), MARGIN)
                at[:MARGIN] += from_left[halo]
                at[CX - MARGIN :] += from_right[halo]
                if t >= PART:
                    turned = at[...].T
                    for h, y in enumerate((t - PART, HALF + PART - 1 - t)):
                        for zg in range(Z // 8):
                            rows = slice(h * Z + zg * 8, h * Z + zg * 8 + 8)
                            flat[pl.ds(zg * 8 * HALF + y, 8, stride=HALF), :] = turned[rows]
            copy = pltpu.make_async_copy(out_s, out_ref.at[:, pl.ds(PART, HALF)], sem)
            copy.start()
            copy.wait()


def spread_rows(part, source, reach, band_z, band_x, *extra):
    partial = (REACHED, CX, CX)
    scratch = [
        pltpu.VMEM((2, GROUP // 2, 2 * CX, 2 * CX), jnp.bfloat16),
        pltpu.VMEM((CLASSES, PART, CX, CX), jnp.float32),
    ]
    if part == 0:
        shapes = [(MARGIN, CX, CX), partial]
        out_specs = [whole(s) for s in shapes]
    else:
        shapes = [(PART, CX, CX), (Z, CY, CX)]
        out_specs = [whole(shapes[0]), pl.BlockSpec(memory_space=pl.ANY)]
        scratch += [
            pltpu.VMEM((HALF + MARGIN, CX, CX), jnp.float32),
            pltpu.VMEM((Z, HALF, CX), jnp.float32),
            pltpu.SemaphoreType.DMA(()),
        ]
    steps = PART // GROUP
    return pl.pallas_call(
        functools.partial(rows_kernel, part),
        grid=(steps,),
        out_shape=[jax.ShapeDtypeStruct(s, jnp.float32) for s in shapes],
        in_specs=[
            pl.BlockSpec((GROUP, CX, 2 * CX), lambda i: (i + part * steps, 0, 0)),
            pl.BlockSpec((GROUP, CX, CX), lambda i: (i + part * steps, 0, 0)),
            whole(band_z.shape),
            whole(band_x.shape),
        ]
        + [whole(a.shape) for a in extra],
        out_specs=out_specs,
        scratch_shapes=scratch,
        compiler_params=pltpu.CompilerParams(vmem_limit_bytes=40 * MIB),
        cost_estimate=pl.CostEstimate(flops=8_000_000_000, bytes_accessed=8_000_000, transcendentals=0),
        name="edge_rows" if part == 0 else "middle_rows",
    )(source, reach, band_z, band_x, *extra)


def pack_kernel(halo, from_left, from_right, up_ref, down_ref, line_s):
    upper = lax.broadcasted_iota(jnp.int32, (64, CX), 1) >= Z
    for j in range(MARGIN):
        rows = pl.ds(MARGIN * j, MARGIN)
        line_s[...] = halo[j]
        line_s[:MARGIN] += from_left[rows]
        line_s[CX - MARGIN :] += from_right[rows]
        one, two = line_s[:64], pltpu.roll(line_s[64:], Z, 1)
        up_ref[j] = jnp.where(upper, one, two)
        down_ref[j] = jnp.where(upper, two, one)


def pack(halo, from_left, from_right):
    return pl.pallas_call(
        pack_kernel,
        out_shape=[jax.ShapeDtypeStruct((MARGIN, 64, CX), jnp.float32)] * 2,
        scratch_shapes=[pltpu.VMEM((CX, CX), jnp.float32)],
        compiler_params=pltpu.CompilerParams(vmem_limit_bytes=8 * MIB),
        name="pack_halo",
    )(halo, from_left, from_right)


def merge_kernel(edge, from_low, from_high, _, out, out_s, sem):
    step = pl.program_id(0)
    upper = lax.broadcasted_iota(jnp.int32, (64, CX), 1) >= Z

    def copies(i):
        return [
            pltpu.make_async_copy(out_s.at[i, h], out.at[:, pl.ds(y, GROUP)], sem.at[i, h])
            for h, y in enumerate((i * GROUP, CY - GROUP - i * GROUP))
        ]

    for i in range(PART // GROUP):

        @pl.when(step == i)
        def _():
            for k in range(GROUP):
                value = edge[k]
                if i * GROUP + k < MARGIN:
                    j = MARGIN - 1 - i * GROUP - k
                    low, high = from_low[j], from_high[j]
                    value = value + jnp.concatenate(
                        [pltpu.roll(jnp.where(upper, low, high), Z, 1), jnp.where(upper, high, low)], axis=0
                    )
                turned = value.T
                for h, y in enumerate((k, GROUP - 1 - k)):
                    flat = out_s.at[i, h].reshape(Z * GROUP, CX)
                    for zg in range(Z // 8):
                        rows = slice(h * Z + zg * 8, h * Z + zg * 8 + 8)
                        flat[pl.ds(zg * 8 * GROUP + y, 8, stride=GROUP), :] = turned[rows]
            for copy in copies(i):
                copy.start()

    @pl.when(step == PART // GROUP - 1)
    def _():
        for i in range(PART // GROUP):
            for copy in copies(i):
                copy.wait()


def merge(edge, from_low, from_high, out):
    return pl.pallas_call(
        merge_kernel,
        grid=(PART // GROUP,),
        out_shape=jax.ShapeDtypeStruct((Z, CY, CX), jnp.float32),
        in_specs=[
            pl.BlockSpec((GROUP, CX, CX), lambda i: (i, 0, 0)),
            whole(from_low.shape),
            whole(from_high.shape),
            pl.BlockSpec(memory_space=pl.ANY),
        ],
        out_specs=pl.BlockSpec(memory_space=pl.ANY),
        scratch_shapes=[
            pltpu.VMEM((PART // GROUP, 2, Z, GROUP, CX), jnp.float32),
            pltpu.SemaphoreType.DMA((PART // GROUP, 2)),
        ],
        input_output_aliases={3: 0},
        compiler_params=pltpu.CompilerParams(vmem_limit_bytes=8 * MIB),
        name="merge_rows",
    )(edge, from_low, from_high, out)


def shifted(value, axis, by):
    length = lax.axis_size(axis)
    return lax.ppermute(value, axis, [(i, i + by) for i in range(length) if 0 <= i + by < length])


def per_device(filtered, upstream, radius_map, brick_class, sharpness, threshold):
    band_z, band_x, band_rim = band_tables()
    source, reach, left, right = rim(
        (brick_class, sharpness, threshold), (filtered, upstream, radius_map), band_z, band_rim
    )
    from_left = shifted(right, "gx", 1)
    from_right = shifted(left, "gx", -1)
    halo, partial = spread_rows(0, source, reach, band_z, band_x)
    up, down = pack(halo, from_left, from_right)
    from_low = shifted(up, "gy", 1)
    from_high = shifted(down, "gy", -1)
    edge, out = spread_rows(1, source, reach, band_z, band_x, partial, from_left, from_right)
    return merge(edge, from_low, from_high, out)


def solution(mesh):
    return jax.shard_map(
        per_device,
        mesh=mesh,
        in_specs=(
            P(None, "gy", "gx"),
            P(None, "gy", "gx"),
            P(None, "gy", "gx"),
            P("gx", "gy"),
            P(),
            P(),
        ),
        out_specs=P(None, "gy", "gx"),
        check_vma=False,
    )
```

time: 443 us -> 56.7 us (0.13); the launches traced: 437 us -> 56.5 us
  matrix products: 257 us -> 0 us
  local copies, waits for them, and re-layouts: 111 us -> 2.83 us
  Pallas kernels: 0 us -> 32 us
  other arithmetic: 28 us -> 0 us
  loops' own time: 9.61 us -> 0 us
  waiting for transfers between devices: 13.6 us -> 4.25 us
    dot_general x33 -> x0, matrix products: 257 us -> none  [the longest x11 111 us: spread_class(): jnp.einsum('zyX,yY->zYX', along_x, band(radius, cells_y, wide_y, margin),...]
    scatter-add x3 -> x0, local copies, waits for them, and re-layouts: 56.2 us -> none  [per_device(): result.at[:, :margin, :].add(below).at[:, cells_y - margin:, :].add(above)]
    pallas_call x0 -> x5, Pallas kernels: none -> 32 us  [the longest x2 17.4 us: spread_rows(): pl.pallas_call(functools.partial(rows_kernel, part), grid=(steps,), out_s...]
    while x66 -> x0, local copies, waits for them, and re-layouts: 24.3 us -> none
    slice x6 -> x0, local copies, waits for them, and re-layouts: 21.1 us -> none  [the longest x2 8.47 us: per_device(): above = from_behind(interior[:, :margin, :], 'gy', -1)]
    add x4 -> x0, other arithmetic: 13.5 us -> none  [the longest x2 13.5 us: per_device(): result.at[:, :margin, :].add(below).at[:, cells_y - margin:, :].add(above)]
    div x1 -> x0, other arithmetic: 13.1 us -> none  [per_device(): source = slope / weight_sum]
    another operation x1 -> x0, loops' own time: 9.61 us -> none  [per_device(): lax.fori_loop(2, upper_class, spread_class, jnp.zeros((cells_z, wide_y, w...]
  transfers between devices with their start and end apart: 4 -> 4, of which waited for: 2 -> 1; matrix products, arithmetic and copies ran while one was open for 10% -> 0% of each run, Pallas kernels for 0% -> 31%
where the time goes in v3:
time: 56.7 us; the launch traced here: 56.5 us
  Pallas kernels  32 us (56%)
  starting transfers between devices  15.2 us (27%)
  waiting for transfers between devices  4.25 us (7%)
  local copies, waits for them, and re-layouts  2.83 us (5%)
  between operations  2.23 us (4%)
    pallas_call x2, Pallas kernels, spread_rows(): pl.pallas_call(functools.partial(rows_kernel, part), grid=(steps,), out_s...  17.4 us
    ppermute x4, starting transfers between devices, shifted(): lax.ppermute(value, axis, [(i, i + by) for i in range(length) if 0 <= i +...  15.2 us
    pallas_call x1, Pallas kernels, rim(): pl.pallas_call(rim_kernel, grid=(groups + 1,), out_shape=[jax.ShapeDtypeS...  13 us
    ppermute x4, waiting for transfers between devices, shifted(): lax.ppermute(value, axis, [(i, i + by) for i in range(length) if 0 <= i +...  4.25 us
    unnamed x10, local copies, waits for them, and re-layouts  2.83 us
    pallas_call x1, Pallas kernels, merge(): pl.pallas_call(merge_kernel, grid=(PART // GROUP,), out_shape=jax.ShapeDt...  1.41 us
  transfers between devices with their start and end apart: 4, of which 1 were waited for; matrix products, arithmetic and copies ran while one was open for 0% of the time, Pallas kernels for 31%

profile of v3, /device:TPU:91, one launch (start us, length us, event | category | flops | bytes accessed | tf_op | source)
XLA Modules:
  0.0 56.5 jit_solution(10280103756194132062)
XLA Ops:
  1.9 0.0 copy-start
  2.0 0.0 copy-start.1
  2.0 13.0 %source_and_rim.1 = (bf16[32,128,256]{2,1,0:T(8,128)(2,1)}, bf16[32,128,128]{2,1,0:T(8,128)(2,1)}, f32[480,128]{1,0:T(8,128)}, f32[480,128]{1,0:T(8,128)}) custom-call(s32[1,1]{1,0:T(1,128)S(6)} %copy.12.class_ref, f32[1]{0:T(128)S(6)} %copy.13.sharp_ref, f32[1]{0:T(128)S(6)} %copy.14.thresh_ref, f32[64,64,128]{2,1,0:T(8,128)} %fil1.1, f32[64,64,128]{2,1,0:T(8,128)} %fil1.1, ...), custom_call_target="tpu_custom_call" | custom-call | flops 4000000000 | bytes 11000000 | tf_op jit(solution)/shard_map/source_and_rim/pallas_call | solution.py:214
  15.0 3.5 %collective-permute-start = (f32[480,128]{1,0:T(8,128)}, f32[480,128]{1,0:T(8,128)S(1)}, u32[]{:S(2)}, u32[]{:S(2)}) collective-permute-start(f32[480,128]{1,0:T(8,128)} %get-tuple-element.18), channel_id=1, source_target_pairs={{0,32},{32,64},{64,96},{96,128},{128,160},{160,192},{192,224},{1,3... | collective-permute-start | bytes 737288 | tf_op jit(solution)/shard_map/ppermute | solution.py:443
  18.5 2.6 %collective-permute-start.1 = (f32[480,128]{1,0:T(8,128)}, f32[480,128]{1,0:T(8,128)S(1)}, u32[]{:S(2)}, u32[]{:S(2)}) collective-permute-start(f32[480,128]{1,0:T(8,128)} %get-tuple-element.19), channel_id=1, source_target_pairs={{32,0},{64,32},{96,64},{128,96},{160,128},{192,160},{224,192},{33,... | collective-permute-start | bytes 737288 | tf_op jit(solution)/shard_map/ppermute | solution.py:443
  21.1 0.0 copy-done
  21.2 0.0 copy-done.1
  21.2 0.0 copy-start.2
  21.2 1.6 %copy-done.2 = bf16[32,128,256]{2,1,0:T(8,128)(2,1)S(1)} copy-done((bf16[32,128,256]{2,1,0:T(8,128)(2,1)S(1)}, bf16[32,128,256]{2,1,0:T(8,128)(2,1)}, u32[]{:S(2)}) %copy-start.2) | copy-done | bytes 2097176
  22.8 0.0 copy-start.3
  22.8 1.2 %copy-done.3 = bf16[32,128,128]{2,1,0:T(8,128)(2,1)S(1)} copy-done((bf16[32,128,128]{2,1,0:T(8,128)(2,1)S(1)}, bf16[32,128,128]{2,1,0:T(8,128)(2,1)}, u32[]{:S(2)}) %copy-start.3) | copy-done | bytes 1048600
  24.0 0.0 copy-start.4
  24.0 7.5 %edge_rows.1 = (f32[11,128,128]{2,1,0:T(8,128)S(1)}, f32[27,128,128]{2,1,0:T(8,128)S(1)}) custom-call(bf16[32,128,256]{2,1,0:T(8,128)(2,1)S(1)} %copy-done.2, bf16[32,128,128]{2,1,0:T(8,128)(2,1)S(1)} %copy-done.3, bf16[11,128,128]{2,1,0:T(8,128)(2,1)S(1)} %copy-done, bf16[11,128,128]{2,1,0:T(8,128)(2,1)S(1)} %copy-done.1), custom_call_target="tpu_custom_call" | custom-call | flops 8000000000 | bytes 8000000 | tf_op jit(solution)/shard_map/edge_rows/pallas_call | solution.py:340
  31.5 0.0 collective-permute-done.refs_5_.from_left
  31.5 0.0 collective-permute-done.1.refs_6_.from_right
  31.6 0.2 pack_halo.1
  31.8 6.9 %collective-permute-start.2 = (f32[11,64,128]{2,1,0:T(8,128)S(1)}, f32[11,64,128]{2,1,0:T(8,128)S(1)}, u32[]{:S(2)}, u32[]{:S(2)}) collective-permute-start(f32[11,64,128]{2,1,0:T(8,128)S(1)} %get-tuple-element.22), channel_id=1, source_target_pairs={{0,1},{1,2},{2,3},{3,4},{4,5},{5,6},{6,7},{7,8},{8,9},{9,10},{10,1... | collective-permute-start | bytes 1081352 | tf_op jit(solution)/shard_map/ppermute | solution.py:443
  38.7 2.1 %collective-permute-start.3 = (f32[11,64,128]{2,1,0:T(8,128)S(1)}, f32[11,64,128]{2,1,0:T(8,128)S(1)}, u32[]{:S(2)}, u32[]{:S(2)}) collective-permute-start(f32[11,64,128]{2,1,0:T(8,128)S(1)} %get-tuple-element.23), channel_id=1, source_target_pairs={{1,0},{2,1},{3,2},{4,3},{5,4},{6,5},{7,6},{8,7},{9,8},{10,9},{11,1... | collective-permute-start | bytes 1081352 | tf_op jit(solution)/shard_map/ppermute | solution.py:443
  40.8 0.0 copy-done.4
  40.8 9.8 %middle_rows.1 = (f32[16,128,128]{2,1,0:T(8,128)S(1)}, f32[64,64,128]{2,1,0:T(8,128)}) custom-call(bf16[32,128,256]{2,1,0:T(8,128)(2,1)S(1)} %copy-done.2, bf16[32,128,128]{2,1,0:T(8,128)(2,1)S(1)} %copy-done.4, bf16[11,128,128]{2,1,0:T(8,128)(2,1)S(1)} %copy-done, bf16[11,128,128]{2,1,0:T(8,128)(2,1)S(1)} %copy-done.1, ...), custom_call_target="tpu_custom_call" | custom-call | flops 8000000000 | bytes 8000000 | tf_op jit(solution)/shard_map/middle_rows/pallas_call | solution.py:340
  50.6 0.0 collective-permute-done.2.from_low
  50.6 4.2 %collective-permute-done.3.from_high = f32[11,64,128]{2,1,0:T(8,128)S(1)} collective-permute-done((f32[11,64,128]{2,1,0:T(8,128)S(1)}, f32[11,64,128]{2,1,0:T(8,128)S(1)}, u32[]{:S(2)}, u32[]{:S(2)}) %collective-permute-start.3) | collective-permute-done | bytes 360480 | tf_op jit(solution)/shard_map/ppermute | solution.py:443
  54.9 1.4 %merge_rows.1 = f32[64,64,128]{2,1,0:T(8,128)} custom-call(f32[16,128,128]{2,1,0:T(8,128)S(1)} %get-tuple-element.20.edge, f32[11,64,128]{2,1,0:T(8,128)S(1)} %collective-permute-done.2.from_low, f32[11,64,128]{2,1,0:T(8,128)S(1)} %collective-permute-done.3.from_high, f32[64,64,128]{2,1,0:T(8,128)} %get-tuple-element.24._), custom_call_target="tpu_custom_call", output_to_operand_aliasing={{}: (3, {})} | custom-call | tf_op jit(solution)/shard_map/merge_rows/pallas_call | solution.py:420
Async XLA Ops:
  1.9 19.2 %copy-start = (bf16[11,128,128]{2,1,0:T(8,128)(2,1)S(1)}, bf16[11,128,128]{2,1,0:T(8,128)(2,1)}, u32[]{:S(2)}) copy-start(bf16[11,128,128]{2,1,0:T(8,128)(2,1)} %constant.6.clone.band_z.refs_2_) | copy-start | bytes 1081348
  2.0 19.2 %copy-start.1 = (bf16[11,128,128]{2,1,0:T(8,128)(2,1)S(1)}, bf16[11,128,128]{2,1,0:T(8,128)(2,1)}, u32[]{:S(2)}) copy-start(bf16[11,128,128]{2,1,0:T(8,128)(2,1)} %constant.7.clone.refs_3_) | copy-start | bytes 1081348
  15.0 16.6 %collective-permute-start = (f32[480,128]{1,0:T(8,128)}, f32[480,128]{1,0:T(8,128)S(1)}, u32[]{:S(2)}, u32[]{:S(2)}) collective-permute-start(f32[480,128]{1,0:T(8,128)} %get-tuple-element.18), channel_id=1, source_target_pairs={{0,32},{32,64},{64,96},{96,128},{128,160},{160,192},{192,224},{1,3... | collective-permute-start | bytes 737288 | tf_op jit(solution)/shard_map/ppermute | solution.py:443
  18.5 13.0 %collective-permute-start.1 = (f32[480,128]{1,0:T(8,128)}, f32[480,128]{1,0:T(8,128)S(1)}, u32[]{:S(2)}, u32[]{:S(2)}) collective-permute-start(f32[480,128]{1,0:T(8,128)} %get-tuple-element.19), channel_id=1, source_target_pairs={{32,0},{64,32},{96,64},{128,96},{160,128},{192,160},{224,192},{33,... | collective-permute-start | bytes 737288 | tf_op jit(solution)/shard_map/ppermute | solution.py:443
  21.2 1.6 %copy-start.2 = (bf16[32,128,256]{2,1,0:T(8,128)(2,1)S(1)}, bf16[32,128,256]{2,1,0:T(8,128)(2,1)}, u32[]{:S(2)}) copy-start(bf16[32,128,256]{2,1,0:T(8,128)(2,1)} %get-tuple-element.15.refs_0_) | copy-start | bytes 6291460
  22.8 1.2 %copy-start.3 = (bf16[32,128,128]{2,1,0:T(8,128)(2,1)S(1)}, bf16[32,128,128]{2,1,0:T(8,128)(2,1)}, u32[]{:S(2)}) copy-start(bf16[32,128,128]{2,1,0:T(8,128)(2,1)} %get-tuple-element.16.refs_1_) | copy-start | bytes 3145732
  24.0 16.8 %copy-start.4 = (bf16[32,128,128]{2,1,0:T(8,128)(2,1)S(1)}, bf16[32,128,128]{2,1,0:T(8,128)(2,1)}, u32[]{:S(2)}) copy-start(bf16[32,128,128]{2,1,0:T(8,128)(2,1)} %get-tuple-element.16.refs_1_) | copy-start | bytes 3145732
  31.8 18.9 %collective-permute-start.2 = (f32[11,64,128]{2,1,0:T(8,128)S(1)}, f32[11,64,128]{2,1,0:T(8,128)S(1)}, u32[]{:S(2)}, u32[]{:S(2)}) collective-permute-start(f32[11,64,128]{2,1,0:T(8,128)S(1)} %get-tuple-element.22), channel_id=1, source_target_pairs={{0,1},{1,2},{2,3},{3,4},{4,5},{5,6},{6,7},{7,8},{8,9},{9,10},{10,1... | collective-permute-start | bytes 1081352 | tf_op jit(solution)/shard_map/ppermute | solution.py:443
  38.7 16.2 %collective-permute-start.3 = (f32[11,64,128]{2,1,0:T(8,128)S(1)}, f32[11,64,128]{2,1,0:T(8,128)S(1)}, u32[]{:S(2)}, u32[]{:S(2)}) collective-permute-start(f32[11,64,128]{2,1,0:T(8,128)S(1)} %get-tuple-element.23), channel_id=1, source_target_pairs={{1,0},{2,1},{3,2},{4,3},{5,4},{6,5},{7,6},{8,7},{9,8},{10,9},{11,1... | collective-permute-start | bytes 1081352 | tf_op jit(solution)/shard_map/ppermute | solution.py:443

commit v4 on v3

--- a/solution.py
+++ b/solution.py
@@ -17,6 +17,9 @@
 PART = HALF // 2
 REACHED = PART + MARGIN
 RIM = 16
+RIM_AHEAD = 4
+MAIN_AHEAD = 2
+MAIN_SLOTS = 4
 HALO_ROWS = 480
 MIB = 1024 * 1024
 
@@ -136,22 +139,23 @@
             pairs = [(pair_s[n, side, :, :CX], pair_s[n, side, :, CX:]) for n, side in both]
             high, low = along_z(c, pairs, [level_s[n, side] for n, side in both], band_z)
             lanes = slice(k // 4 * CX, k // 4 * CX + CX)
-            grown_s[c % 2, :CX, lanes] = high
-            grown_s[c % 2, CX:, lanes] = low
+            grown_s[c, :CX, lanes] = high
+            grown_s[c, CX:, lanes] = low
 
     def rim_x(c):
         both = jnp.concatenate([band_rim[c], band_rim[c]], axis=1)
-        moved = jnp.dot(both, grown_s[c % 2], preferred_element_type=jnp.float32)
+        moved = jnp.dot(both, grown_s[c], preferred_element_type=jnp.float32)
         for k in range(GROUP):
             lanes = slice(k // 4 * CX, k // 4 * CX + CX)
             rows = slice(k % 4 * 2 * RIM, k % 4 * 2 * RIM + 2 * RIM)
             smooth_s[c, (step - 1) * GROUP + k] = moved[rows, lanes]
 
     def classes(pair_s, level_s, beside):
-        rim_z(0, pair_s, level_s)
+        for c in range(RIM_AHEAD):
+            rim_z(c, pair_s, level_s)
         for c in range(CLASSES):
-            if c + 1 < CLASSES:
-                rim_z(c + 1, pair_s, level_s)
+            if c + RIM_AHEAD < CLASSES:
+                rim_z(c + RIM_AHEAD, pair_s, level_s)
             beside(c)
             rim_x(c)
 
@@ -234,11 +238,11 @@
             pltpu.VMEM((GROUP, 2, RIM, 2 * CX), jnp.bfloat16),
             pltpu.VMEM((GROUP, 2, RIM, CX), jnp.bfloat16),
             pltpu.VMEM((GROUP, 2, RIM, CX), jnp.bfloat16),
-            pltpu.VMEM((2, 2 * CX, 2 * CX), jnp.bfloat16),
+            pltpu.VMEM((CLASSES, 2 * CX, 2 * CX), jnp.bfloat16),
             pltpu.VMEM((CLASSES, HALF, 2 * RIM, CX), jnp.float32),
             pltpu.VMEM((HALF + 2 * MARGIN, 2 * RIM, CX), jnp.float32),
         ],
-        compiler_params=pltpu.CompilerParams(vmem_limit_bytes=60 * MIB),
+        compiler_params=pltpu.CompilerParams(vmem_limit_bytes=24 * MIB),
         cost_estimate=pl.CostEstimate(flops=4_000_000_000, bytes_accessed=11_000_000, transcendentals=524288),
         name="source_and_rim",
     )(*scalars, *[a for a in fields for _ in (0, 1)], band_z, band_rim)
@@ -253,6 +257,7 @@
         part_ref, from_left, from_right, edge_ref, out_ref = refs[4:9]
         grown_s, smooth_s, ext_s, out_s, sem = refs[9:]
     step = pl.program_id(0)
+    start = part * PART
 
     def main_z(c):
         for k in range(0, GROUP, 2):
@@ -260,46 +265,74 @@
             high, low = along_z(c, pairs, [reach_ref[n] for n in (k, k + 1)], band_z)
             for n in (0, 1):
                 here = slice(n * CX, n * CX + CX)
-                grown_s[c % 2, k // 2, :CX, here] = high[here]
-                grown_s[c % 2, k // 2, CX:, here] = low[here]
-
-    def main_x(c):
+                grown_s[c % MAIN_SLOTS, k // 2, :CX, here] = high[here]
+                grown_s[c % MAIN_SLOTS, k // 2, CX:, here] = low[here]
+
+    def main_x(c, group):
         both = jnp.concatenate([band_x[c], band_x[c]], axis=1)
         for k in range(GROUP // 2):
-            moved = jnp.dot(both, grown_s[c % 2, k], preferred_element_type=jnp.float32)
-            smooth_s[c, step * GROUP + 2 * k] = moved[:, :CX]
-            smooth_s[c, step * GROUP + 2 * k + 1] = moved[:, CX:]
-
-    main_z(0)
-    for c in range(CLASSES):
-        if c + 1 < CLASSES:
-            main_z(c + 1)
-        main_x(c)
-
-    @pl.when(step == PART // GROUP - 1)
-    def _():
-        start = part * PART
-
-        def tile(k, _):
-            rows = pl.ds(pl.multiple_of(k * 8, 8), 8)
-
-            def keep(t, value):
-                if part == 1:
-                    ext_s[t, rows] = value
-                elif t < 0:
-                    halo_ref[t + MARGIN, rows] = value
-                else:
-                    part_ref[t, rows] = value
-
-            total = {t: part_ref[t, rows] for t in range(start - MARGIN, REACHED)} if part == 1 else {}
-            load = lambda radius, t: smooth_s[radius - 2, t - start, rows]
-            spread_y(load, range(start, start + PART), total, keep)
-            return 0
-
-        lax.fori_loop(0, CX // 8, tile, 0)
+            moved = jnp.dot(both, grown_s[c % MAIN_SLOTS, k], preferred_element_type=jnp.float32)
+            smooth_s[c, group * GROUP + 2 * k] = moved[:, :CX]
+            smooth_s[c, group * GROUP + 2 * k + 1] = moved[:, CX:]
+
+    def classes(group, beside):
+        for c in range(MAIN_AHEAD):
+            main_z(c)
+        for c in range(CLASSES):
+            if c + MAIN_AHEAD < CLASSES:
+                main_z(c + MAIN_AHEAD)
+            beside(c)
+            main_x(c, group)
+
+    def tile(group, rows):
+        first = start + group * GROUP
+
+        def place(t):
+            if part == 1:
+                return ext_s, t
+            return (halo_ref, t + MARGIN) if t < 0 else (part_ref, t)
+
+        def keep(t, value):
+            ref, at = place(t)
+            ref[at, rows] = value
+
+        total = {}
+        for t in range(first - MARGIN, first + MARGIN):
+            if group > 0:
+                ref, at = place(t)
+                total[t] = ref[at, rows]
+            elif part == 1 and t < REACHED:
+                total[t] = part_ref[t, rows]
+        load = lambda radius, t: smooth_s[radius - 2, t - start, rows]
+        spread_y(load, range(first, first + GROUP), total, keep)
+
+    tiles = CX // 8
+
+    def tiles_beside(c):
+        for k in range(c * tiles // CLASSES, (c + 1) * tiles // CLASSES):
+            tile(0, slice(k * 8, k * 8 + 8))
+
+    @pl.when(step == 0)
+    def _():
+        classes(0, lambda c: None)
+
+    @pl.when(step == 1)
+    def _():
+        classes(1, tiles_beside)
+
+        @pl.loop(0, tiles)
+        def _(k):
+            tile(1, pl.ds(pl.multiple_of(k * 8, 8), 8))
+
         if part == 1:
-            flat = out_s.reshape(Z * PART * 2, CX)
-            for t in range(HALF):
+            flat = out_s.reshape(Z * HALF, CX)
+            copies = [
+                pltpu.make_async_copy(
+                    out_s.at[:, pl.ds(y, GROUP)], out_ref.at[:, pl.ds(PART + y, GROUP)], sem.at[n]
+                )
+                for n, y in enumerate((0, HALF - GROUP, GROUP, HALF - 2 * GROUP))
+            ]
+            for t in [*range(PART, HALF), *range(PART)]:
                 at = edge_ref.at[t] if t < PART else ext_s.at[t]
                 if t < PART:
                     at[...] = part_ref[t] if t < start - MARGIN else ext_s[t]
@@ -314,15 +347,17 @@
                         for zg in range(Z // 8):
                             rows = slice(h * Z + zg * 8, h * Z + zg * 8 + 8)
                             flat[pl.ds(zg * 8 * HALF + y, 8, stride=HALF), :] = turned[rows]
-            copy = pltpu.make_async_copy(out_s, out_ref.at[:, pl.ds(PART, HALF)], sem)
-            copy.start()
-            copy.wait()
+                if t in (PART + GROUP - 1, HALF - 1):
+                    for copy in copies[:2] if t < HALF - 1 else copies[2:]:
+                        copy.start()
+            for copy in copies:
+                copy.wait()
 
 
 def spread_rows(part, source, reach, band_z, band_x, *extra):
     partial = (REACHED, CX, CX)
     scratch = [
-        pltpu.VMEM((2, GROUP // 2, 2 * CX, 2 * CX), jnp.bfloat16),
+        pltpu.VMEM((MAIN_SLOTS, GROUP // 2, 2 * CX, 2 * CX), jnp.bfloat16),
         pltpu.VMEM((CLASSES, PART, CX, CX), jnp.float32),
     ]
     if part == 0:
@@ -334,7 +369,7 @@
         scratch += [
             pltpu.VMEM((HALF + MARGIN, CX, CX), jnp.float32),
             pltpu.VMEM((Z, HALF, CX), jnp.float32),
-            pltpu.SemaphoreType.DMA(()),
+            pltpu.SemaphoreType.DMA((4,)),
         ]
     steps = PART // GROUP
     return pl.pallas_call(
@@ -445,8 +480,10 @@
 
 def per_device(filtered, upstream, radius_map, brick_class, sharpness, threshold):
     band_z, band_x, band_rim = band_tables()
+    in_hbm = lambda a: pltpu.with_memory_space_constraint(a, pltpu.HBM)
+    fields = [in_hbm(a) for a in (filtered, upstream, radius_map)]
     source, reach, left, right = rim(
-        (brick_class, sharpness, threshold), (filtered, upstream, radius_map), band_z, band_rim
+        (brick_class, sharpness, threshold), fields, in_hbm(band_z), in_hbm(band_rim)
     )
     from_left = shifted(right, "gx", 1)
     from_right = shifted(left, "gx", -1)

time: 56.7 us -> 52.5 us (0.926)
  Pallas kernels: 32 us -> 28.8 us
  local copies, waits for them, and re-layouts: 2.83 us -> 0.01 us
  waiting for transfers between devices: 4.25 us -> 5.82 us
    pallas_call x1, Pallas kernels: 13 us -> 9.7 us  [rim(): pl.pallas_call(rim_kernel, grid=(groups + 1,), out_shape=[jax.ShapeDtypeS...]
    unnamed x10 -> x4, local copies, waits for them, and re-layouts: 2.83 us -> 0.01 us
    ppermute x4, waiting for transfers between devices: 4.25 us -> 5.82 us  [shifted(): lax.ppermute(value, axis, [(i, i + by) for i in range(length) if 0 <= i +...]
  transfers between devices with their start and end apart: 4 -> 4, of which waited for: 1 -> 2; matrix products, arithmetic and copies ran while one was open for 0% -> 0% of each run, Pallas kernels for 31% -> 33%
where the time goes in v4:
time: 52.5 us; the launch traced here: 52.3 us
  Pallas kernels  28.8 us (55%)
  starting transfers between devices  15.5 us (30%)
  waiting for transfers between devices  5.82 us (11%)
  between operations  2.21 us (4%)
    pallas_call x2, Pallas kernels, spread_rows(): pl.pallas_call(functools.partial(rows_kernel, part), grid=(steps,), out_s...  17.4 us
    ppermute x4, starting transfers between devices, shifted(): lax.ppermute(value, axis, [(i, i + by) for i in range(length) if 0 <= i +...  15.5 us
    pallas_call x1, Pallas kernels, rim(): pl.pallas_call(rim_kernel, grid=(groups + 1,), out_shape=[jax.ShapeDtypeS...  9.7 us
    ppermute x4, waiting for transfers between devices, shifted(): lax.ppermute(value, axis, [(i, i + by) for i in range(length) if 0 <= i +...  5.82 us
    pallas_call x1, Pallas kernels, merge(): pl.pallas_call(merge_kernel, grid=(PART // GROUP,), out_shape=jax.ShapeDt...  1.41 us
  transfers between devices with their start and end apart: 4, of which 2 were waited for; matrix products, arithmetic and copies ran while one was open for 0% of the time, Pallas kernels for 33%

profile of v4, /device:TPU:91, one launch (start us, length us, event | category | flops | bytes accessed | tf_op | source)
XLA Modules:
  0.0 52.3 jit_solution(3438743313097127221)
XLA Ops:
  1.9 0.0 copy-start
  2.0 0.0 copy-start.1
  2.0 9.7 %source_and_rim.1 = (bf16[32,128,256]{2,1,0:T(8,128)(2,1)S(1)}, bf16[32,128,128]{2,1,0:T(8,128)(2,1)S(1)}, f32[480,128]{1,0:T(8,128)S(1)}, f32[480,128]{1,0:T(8,128)S(1)}) custom-call(s32[1,1]{1,0:T(1,128)S(6)} %copy.12.class_ref, f32[1]{0:T(128)S(6)} %copy.13.sharp_ref, f32[1]{0:T(128)S(6)} %copy.14.thresh_ref, f32[64,64,128]{2,1,0:T(8,128)} %fil1.1, ...), custom_call_target="tpu_custom_call" | custom-call | flops 4000000000 | bytes 11000000 | tf_op jit(solution)/shard_map/source_and_rim/pallas_call | solution.py:218
  11.7 3.5 %collective-permute-start = (f32[480,128]{1,0:T(8,128)S(1)}, f32[480,128]{1,0:T(8,128)S(1)}, u32[]{:S(2)}, u32[]{:S(2)}) collective-permute-start(f32[480,128]{1,0:T(8,128)S(1)} %get-tuple-element.18), channel_id=1, source_target_pairs={{0,32},{32,64},{64,96},{96,128},{128,160},{160,192},{192,224},{1,3... | collective-permute-start | bytes 737288 | tf_op jit(solution)/shard_map/ppermute | solution.py:478
  15.2 2.6 %collective-permute-start.1 = (f32[480,128]{1,0:T(8,128)S(1)}, f32[480,128]{1,0:T(8,128)S(1)}, u32[]{:S(2)}, u32[]{:S(2)}) collective-permute-start(f32[480,128]{1,0:T(8,128)S(1)} %get-tuple-element.19), channel_id=1, source_target_pairs={{32,0},{64,32},{96,64},{128,96},{160,128},{192,160},{224,192},{33,... | collective-permute-start | bytes 737288 | tf_op jit(solution)/shard_map/ppermute | solution.py:478
  17.9 0.0 copy-done
  17.9 0.0 copy-done.1
  17.9 7.6 %edge_rows.1 = (f32[11,128,128]{2,1,0:T(8,128)S(1)}, f32[27,128,128]{2,1,0:T(8,128)S(1)}) custom-call(bf16[32,128,256]{2,1,0:T(8,128)(2,1)S(1)} %get-tuple-element.15.refs_0_, bf16[32,128,128]{2,1,0:T(8,128)(2,1)S(1)} %get-tuple-element.16.refs_1_, bf16[11,128,128]{2,1,0:T(8,128)(2,1)S(1)} %copy-done, bf16[11,128,128]{2,1,0:T(8,128)(2,1)S(1)} %copy-done.1), custom_call_target="tpu_custom_call" | custom-call | flops 8000000000 | bytes 8000000 | tf_op jit(solution)/shard_map/edge_rows/pallas_call | solution.py:375
  25.5 0.0 collective-permute-done.refs_5_.from_left
  25.5 1.1 %collective-permute-done.1.refs_6_.from_right = f32[480,128]{1,0:T(8,128)S(1)} collective-permute-done((f32[480,128]{1,0:T(8,128)S(1)}, f32[480,128]{1,0:T(8,128)S(1)}, u32[]{:S(2)}, u32[]{:S(2)}) %collective-permute-start.1) | collective-permute-done | bytes 245792 | tf_op jit(solution)/shard_map/ppermute | solution.py:478
  26.6 0.2 pack_halo.1
  26.8 7.2 %collective-permute-start.2 = (f32[11,64,128]{2,1,0:T(8,128)S(1)}, f32[11,64,128]{2,1,0:T(8,128)S(1)}, u32[]{:S(2)}, u32[]{:S(2)}) collective-permute-start(f32[11,64,128]{2,1,0:T(8,128)S(1)} %get-tuple-element.22), channel_id=1, source_target_pairs={{0,1},{1,2},{2,3},{3,4},{4,5},{5,6},{6,7},{7,8},{8,9},{9,10},{10,1... | collective-permute-start | bytes 1081352 | tf_op jit(solution)/shard_map/ppermute | solution.py:478
  34.0 2.1 %collective-permute-start.3 = (f32[11,64,128]{2,1,0:T(8,128)S(1)}, f32[11,64,128]{2,1,0:T(8,128)S(1)}, u32[]{:S(2)}, u32[]{:S(2)}) collective-permute-start(f32[11,64,128]{2,1,0:T(8,128)S(1)} %get-tuple-element.23), channel_id=1, source_target_pairs={{1,0},{2,1},{3,2},{4,3},{5,4},{6,5},{7,6},{8,7},{9,8},{10,9},{11,1... | collective-permute-start | bytes 1081352 | tf_op jit(solution)/shard_map/ppermute | solution.py:478
  36.1 9.9 %middle_rows.1 = (f32[16,128,128]{2,1,0:T(8,128)S(1)}, f32[64,64,128]{2,1,0:T(8,128)}) custom-call(bf16[32,128,256]{2,1,0:T(8,128)(2,1)S(1)} %get-tuple-element.15.refs_0_, bf16[32,128,128]{2,1,0:T(8,128)(2,1)S(1)} %get-tuple-element.16.refs_1_, bf16[11,128,128]{2,1,0:T(8,128)(2,1)S(1)} %copy-done, bf16[11,128,128]{2,1,0:T(8,128)(2,1)S(1)} %copy-done.1, ...), custom_call_target="tpu_custom_call" | custom-call | flops 8000000000 | bytes 8000000 | tf_op jit(solution)/shard_map/middle_rows/pallas_call | solution.py:375
  46.0 0.0 collective-permute-done.2.from_low
  46.0 4.7 %collective-permute-done.3.from_high = f32[11,64,128]{2,1,0:T(8,128)S(1)} collective-permute-done((f32[11,64,128]{2,1,0:T(8,128)S(1)}, f32[11,64,128]{2,1,0:T(8,128)S(1)}, u32[]{:S(2)}, u32[]{:S(2)}) %collective-permute-start.3) | collective-permute-done | bytes 360480 | tf_op jit(solution)/shard_map/ppermute | solution.py:478
  50.7 1.4 %merge_rows.1 = f32[64,64,128]{2,1,0:T(8,128)} custom-call(f32[16,128,128]{2,1,0:T(8,128)S(1)} %get-tuple-element.20.edge, f32[11,64,128]{2,1,0:T(8,128)S(1)} %collective-permute-done.2.from_low, f32[11,64,128]{2,1,0:T(8,128)S(1)} %collective-permute-done.3.from_high, f32[64,64,128]{2,1,0:T(8,128)} %get-tuple-element.24._), custom_call_target="tpu_custom_call", output_to_operand_aliasing={{}: (3, {})} | custom-call | tf_op jit(solution)/shard_map/merge_rows/pallas_call | solution.py:455
Async XLA Ops:
  1.9 15.9 %copy-start = (bf16[11,128,128]{2,1,0:T(8,128)(2,1)S(1)}, bf16[11,128,128]{2,1,0:T(8,128)(2,1)}, u32[]{:S(2)}) copy-start(bf16[11,128,128]{2,1,0:T(8,128)(2,1)} %constant.6.clone.band_z.refs_2_) | copy-start | bytes 1081348
  2.0 15.9 %copy-start.1 = (bf16[11,128,128]{2,1,0:T(8,128)(2,1)S(1)}, bf16[11,128,128]{2,1,0:T(8,128)(2,1)}, u32[]{:S(2)}) copy-start(bf16[11,128,128]{2,1,0:T(8,128)(2,1)} %constant.7.clone.refs_3_) | copy-start | bytes 1081348
  11.7 13.8 %collective-permute-start = (f32[480,128]{1,0:T(8,128)S(1)}, f32[480,128]{1,0:T(8,128)S(1)}, u32[]{:S(2)}, u32[]{:S(2)}) collective-permute-start(f32[480,128]{1,0:T(8,128)S(1)} %get-tuple-element.18), channel_id=1, source_target_pairs={{0,32},{32,64},{64,96},{96,128},{128,160},{160,192},{192,224},{1,3... | collective-permute-start | bytes 737288 | tf_op jit(solution)/shard_map/ppermute | solution.py:478
  15.2 11.4 %collective-permute-start.1 = (f32[480,128]{1,0:T(8,128)S(1)}, f32[480,128]{1,0:T(8,128)S(1)}, u32[]{:S(2)}, u32[]{:S(2)}) collective-permute-start(f32[480,128]{1,0:T(8,128)S(1)} %get-tuple-element.19), channel_id=1, source_target_pairs={{32,0},{64,32},{96,64},{128,96},{160,128},{192,160},{224,192},{33,... | collective-permute-start | bytes 737288 | tf_op jit(solution)/shard_map/ppermute | solution.py:478
  26.8 19.2 %collective-permute-start.2 = (f32[11,64,128]{2,1,0:T(8,128)S(1)}, f32[11,64,128]{2,1,0:T(8,128)S(1)}, u32[]{:S(2)}, u32[]{:S(2)}) collective-permute-start(f32[11,64,128]{2,1,0:T(8,128)S(1)} %get-tuple-element.22), channel_id=1, source_target_pairs={{0,1},{1,2},{2,3},{3,4},{4,5},{5,6},{6,7},{7,8},{8,9},{9,10},{10,1... | collective-permute-start | bytes 1081352 | tf_op jit(solution)/shard_map/ppermute | solution.py:478
  34.0 16.7 %collective-permute-start.3 = (f32[11,64,128]{2,1,0:T(8,128)S(1)}, f32[11,64,128]{2,1,0:T(8,128)S(1)}, u32[]{:S(2)}, u32[]{:S(2)}) collective-permute-start(f32[11,64,128]{2,1,0:T(8,128)S(1)} %get-tuple-element.23), channel_id=1, source_target_pairs={{1,0},{2,1},{3,2},{4,3},{5,4},{6,5},{7,6},{8,7},{9,8},{10,9},{11,1... | collective-permute-start | bytes 1081352 | tf_op jit(solution)/shard_map/ppermute | solution.py:478

commit v5 on v4

--- a/solution.py
+++ b/solution.py
@@ -86,7 +86,7 @@
 
 def rim_kernel(
     class_ref, sharp_ref, thresh_ref, fil0, fil1, ups0, ups1, rad0, rad1, band_z, band_rim,
-    source_ref, reach_ref, left_ref, right_ref, pair_a, pair_b, level_a, level_b, grown_s, smooth_s, ext_s,
+    source_ref, reach_ref, near_ref, next_ref, pair_a, pair_b, level_a, level_b, grown_s, smooth_s, ext_s,
 ):
     fil, ups, rad = (
         [ref.reshape(Z * GROUP, CX) for ref in pair] for pair in ((fil0, fil1), (ups0, ups1), (rad0, rad1))
@@ -200,9 +200,11 @@
             full = ext_s[t + MARGIN]
             if t >= HALF - MARGIN:
                 full = full + pltpu.roll(ext_s[2 * HALF - 1 - t + MARGIN], Z, 1)
-            left_ref[pl.ds(MARGIN * (t + MARGIN), MARGIN)] = full[:MARGIN]
-            right_ref[pl.ds(MARGIN * (t + MARGIN), MARGIN)] = full[RIM : RIM + MARGIN]
-        for ref in (left_ref, right_ref):
+            left, right = full[:RIM], full[RIM:]
+            rows = pl.ds(MARGIN * (t + MARGIN), MARGIN)
+            near_ref[rows] = jnp.where(col % 2 == 0, right, left)[:MARGIN]
+            next_ref[rows] = jnp.where(col % 2 == 0, left, right)[:MARGIN]
+        for ref in (near_ref, next_ref):
             spare = HALO_ROWS - MARGIN * (HALF + MARGIN)
             ref[pl.ds(HALO_ROWS - spare, spare)] = jnp.zeros((spare, CX), jnp.float32)
 
@@ -248,13 +250,18 @@
     )(*scalars, *[a for a in fields for _ in (0, 1)], band_z, band_rim)
 
 
+def sides(axis, near, after):
+    even = lax.axis_index(axis) % 2 == 0
+    return jnp.where(even, after, near), jnp.where(even, near, after)
+
+
 def rows_kernel(part, *refs):
     source_ref, reach_ref, band_z, band_x = refs[:4]
     if part == 0:
         halo_ref, part_ref = refs[4:6]
         grown_s, smooth_s = refs[6:]
     else:
-        part_ref, from_left, from_right, edge_ref, out_ref = refs[4:9]
+        part_ref, x_near, x_next, edge_ref, out_ref = refs[4:9]
         grown_s, smooth_s, ext_s, out_s, sem = refs[9:]
     step = pl.program_id(0)
     start = part * PART
@@ -339,8 +346,9 @@
                 elif t >= HALF - MARGIN:
                     at[...] += pltpu.roll(ext_s[2 * HALF - 1 - t], Z, 1)
                 halo = pl.ds(MARGIN * (t + MARGIN), MARGIN)
-                at[:MARGIN] += from_left[halo]
-                at[CX - MARGIN :] += from_right[halo]
+                from_left, from_right = sides("gx", x_near[halo], x_next[halo])
+                at[:MARGIN] += from_left
+                at[CX - MARGIN :] += from_right
                 if t >= PART:
                     turned = at[...].T
                     for h, y in enumerate((t - PART, HALF + PART - 1 - t)):
@@ -391,29 +399,29 @@
     )(source, reach, band_z, band_x, *extra)
 
 
-def pack_kernel(halo, from_left, from_right, up_ref, down_ref, line_s):
+def pack_kernel(halo, x_near, x_next, near_ref, next_ref, line_s):
     upper = lax.broadcasted_iota(jnp.int32, (64, CX), 1) >= Z
     for j in range(MARGIN):
         rows = pl.ds(MARGIN * j, MARGIN)
         line_s[...] = halo[j]
-        line_s[:MARGIN] += from_left[rows]
-        line_s[CX - MARGIN :] += from_right[rows]
+        from_left, from_right = sides("gx", x_near[rows], x_next[rows])
+        line_s[:MARGIN] += from_left
+        line_s[CX - MARGIN :] += from_right
         one, two = line_s[:64], pltpu.roll(line_s[64:], Z, 1)
-        up_ref[j] = jnp.where(upper, one, two)
-        down_ref[j] = jnp.where(upper, two, one)
-
-
-def pack(halo, from_left, from_right):
+        next_ref[j], near_ref[j] = sides("gy", jnp.where(upper, one, two), jnp.where(upper, two, one))
+
+
+def pack(halo, x_near, x_next):
     return pl.pallas_call(
         pack_kernel,
         out_shape=[jax.ShapeDtypeStruct((MARGIN, 64, CX), jnp.float32)] * 2,
         scratch_shapes=[pltpu.VMEM((CX, CX), jnp.float32)],
         compiler_params=pltpu.CompilerParams(vmem_limit_bytes=8 * MIB),
         name="pack_halo",
-    )(halo, from_left, from_right)
-
-
-def merge_kernel(edge, from_low, from_high, _, out, out_s, sem):
+    )(halo, x_near, x_next)
+
+
+def merge_kernel(edge, y_near, y_next, _, out, out_s, sem):
     step = pl.program_id(0)
     upper = lax.broadcasted_iota(jnp.int32, (64, CX), 1) >= Z
 
@@ -431,7 +439,7 @@
                 value = edge[k]
                 if i * GROUP + k < MARGIN:
                     j = MARGIN - 1 - i * GROUP - k
-                    low, high = from_low[j], from_high[j]
+                    low, high = sides("gy", y_near[j], y_next[j])
                     value = value + jnp.concatenate(
                         [pltpu.roll(jnp.where(upper, low, high), Z, 1), jnp.where(upper, high, low)], axis=0
                     )
@@ -451,15 +459,15 @@
                 copy.wait()
 
 
-def merge(edge, from_low, from_high, out):
+def merge(edge, y_near, y_next, out):
     return pl.pallas_call(
         merge_kernel,
         grid=(PART // GROUP,),
         out_shape=jax.ShapeDtypeStruct((Z, CY, CX), jnp.float32),
         in_specs=[
             pl.BlockSpec((GROUP, CX, CX), lambda i: (i, 0, 0)),
-            whole(from_low.shape),
-            whole(from_high.shape),
+            whole(y_near.shape),
+            whole(y_next.shape),
             pl.BlockSpec(memory_space=pl.ANY),
         ],
         out_specs=pl.BlockSpec(memory_space=pl.ANY),
@@ -470,29 +478,29 @@
         input_output_aliases={3: 0},
         compiler_params=pltpu.CompilerParams(vmem_limit_bytes=8 * MIB),
         name="merge_rows",
-    )(edge, from_low, from_high, out)
-
-
-def shifted(value, axis, by):
-    length = lax.axis_size(axis)
-    return lax.ppermute(value, axis, [(i, i + by) for i in range(length) if 0 <= i + by < length])
+    )(edge, y_near, y_next, out)
+
+
+def swapped(value, axis, first):
+    pairs = [(i, i + 1) for i in range(first, lax.axis_size(axis) - 1, 2)]
+    return lax.ppermute(value, axis, pairs + [(b, a) for a, b in pairs])
 
 
 def per_device(filtered, upstream, radius_map, brick_class, sharpness, threshold):
     band_z, band_x, band_rim = band_tables()
     in_hbm = lambda a: pltpu.with_memory_space_constraint(a, pltpu.HBM)
     fields = [in_hbm(a) for a in (filtered, upstream, radius_map)]
-    source, reach, left, right = rim(
+    source, reach, x_near, x_next = rim(
         (brick_class, sharpness, threshold), fields, in_hbm(band_z), in_hbm(band_rim)
     )
-    from_left = shifted(right, "gx", 1)
-    from_right = shifted(left, "gx", -1)
+    x_next = swapped(x_next, "gx", 1)
+    x_near = swapped(x_near, "gx", 0)
     halo, partial = spread_rows(0, source, reach, band_z, band_x)
-    up, down = pack(halo, from_left, from_right)
-    from_low = shifted(up, "gy", 1)
-    from_high = shifted(down, "gy", -1)
-    edge, out = spread_rows(1, source, reach, band_z, band_x, partial, from_left, from_right)
-    return merge(edge, from_low, from_high, out)
+    y_near, y_next = pack(halo, x_near, x_next)
+    y_next = swapped(y_next, "gy", 1)
+    y_near = swapped(y_near, "gy", 0)
+    edge, out = spread_rows(1, source, reach, band_z, band_x, partial, x_near, x_next)
+    return merge(edge, y_near, y_next, out)
 
 
 def solution(mesh):

time: 52.5 us -> 44.4 us (0.85)
  starting transfers between devices: 15.5 us -> 10.7 us
  waiting for transfers between devices: 5.82 us -> 2.56 us
    ppermute x4, starting transfers between devices: 15.5 us -> 10.7 us  [swapped(): return lax.ppermute(value, axis, pairs + [(b, a) for a, b in pairs])]
    ppermute x4, waiting for transfers between devices: 5.82 us -> 2.56 us  [swapped(): return lax.ppermute(value, axis, pairs + [(b, a) for a, b in pairs])]
  transfers between devices with their start and end apart: 4 -> 4, of which waited for: 2 -> 2; matrix products, arithmetic and copies ran while one was open for 0% -> 0% of each run, Pallas kernels for 33% -> 39%
where the time goes in v5:
time: 44.4 us; the launch traced here: 44.2 us
  Pallas kernels  28.8 us (65%)
  starting transfers between devices  10.7 us (24%)
  waiting for transfers between devices  2.56 us (6%)
  between operations  2.19 us (5%)
    pallas_call x2, Pallas kernels, spread_rows(): pl.pallas_call(functools.partial(rows_kernel, part), grid=(steps,), out_s...  17.4 us
    ppermute x4, starting transfers between devices, swapped(): return lax.ppermute(value, axis, pairs + [(b, a) for a, b in pairs])  10.7 us
    pallas_call x1, Pallas kernels, rim(): pl.pallas_call(rim_kernel, grid=(groups + 1,), out_shape=[jax.ShapeDtypeS...  9.7 us
    ppermute x4, waiting for transfers between devices, swapped(): return lax.ppermute(value, axis, pairs + [(b, a) for a, b in pairs])  2.56 us
    pallas_call x1, Pallas kernels, merge(): pl.pallas_call(merge_kernel, grid=(PART // GROUP,), out_shape=jax.ShapeDt...  1.43 us
  transfers between devices with their start and end apart: 4, of which 2 were waited for; matrix products, arithmetic and copies ran while one was open for 0% of the time, Pallas kernels for 39%

profile of v5, /device:TPU:91, one launch (start us, length us, event | category | flops | bytes accessed | tf_op | source)
XLA Modules:
  0.0 44.2 jit_solution(9696482099799697605)
XLA Ops:
  1.9 0.0 copy-start
  2.0 0.0 copy-start.1
  2.0 9.7 %source_and_rim.1 = (bf16[32,128,256]{2,1,0:T(8,128)(2,1)S(1)}, bf16[32,128,128]{2,1,0:T(8,128)(2,1)S(1)}, f32[480,128]{1,0:T(8,128)S(1)}, f32[480,128]{1,0:T(8,128)S(1)}) custom-call(s32[1,1]{1,0:T(1,128)S(6)} %copy.12.class_ref, f32[1]{0:T(128)S(6)} %copy.13.sharp_ref, f32[1]{0:T(128)S(6)} %copy.14.thresh_ref, f32[64,64,128]{2,1,0:T(8,128)} %fil1.1, ...), custom_call_target="tpu_custom_call" | custom-call | flops 4000000000 | bytes 11000000 | tf_op jit(solution)/shard_map/source_and_rim/pallas_call | solution.py:220
  11.7 1.7 %collective-permute-start = (f32[480,128]{1,0:T(8,128)S(1)}, f32[480,128]{1,0:T(8,128)S(1)}, u32[]{:S(2)}, u32[]{:S(2)}) collective-permute-start(f32[480,128]{1,0:T(8,128)S(1)} %get-tuple-element.18), channel_id=1, source_target_pairs={{0,32},{64,96},{128,160},{192,224},{32,0},{96,64},{160,128},{224,1... | collective-permute-start | bytes 737288 | tf_op jit(solution)/shard_map/ppermute | solution.py:486
  13.4 1.9 %collective-permute-start.1 = (f32[480,128]{1,0:T(8,128)S(1)}, f32[480,128]{1,0:T(8,128)S(1)}, u32[]{:S(2)}, u32[]{:S(2)}) collective-permute-start(f32[480,128]{1,0:T(8,128)S(1)} %get-tuple-element.19), channel_id=1, source_target_pairs={{32,64},{96,128},{160,192},{64,32},{128,96},{192,160},{33,65},{97,... | collective-permute-start | bytes 737288 | tf_op jit(solution)/shard_map/ppermute | solution.py:486
  15.3 0.0 copy-done
  15.3 0.0 copy-done.1
  15.3 7.6 %edge_rows.1 = (f32[11,128,128]{2,1,0:T(8,128)S(1)}, f32[27,128,128]{2,1,0:T(8,128)S(1)}) custom-call(bf16[32,128,256]{2,1,0:T(8,128)(2,1)S(1)} %get-tuple-element.15.refs_0_, bf16[32,128,128]{2,1,0:T(8,128)(2,1)S(1)} %get-tuple-element.16.refs_1_, bf16[11,128,128]{2,1,0:T(8,128)(2,1)S(1)} %copy-done, bf16[11,128,128]{2,1,0:T(8,128)(2,1)S(1)} %copy-done.1), custom_call_target="tpu_custom_call" | custom-call | flops 8000000000 | bytes 8000000 | tf_op jit(solution)/shard_map/edge_rows/pallas_call | solution.py:383
  22.9 0.0 collective-permute-done.refs_5_.x_near
  22.9 1.3 %collective-permute-done.1.refs_6_.x_next = f32[480,128]{1,0:T(8,128)S(1)} collective-permute-done((f32[480,128]{1,0:T(8,128)S(1)}, f32[480,128]{1,0:T(8,128)S(1)}, u32[]{:S(2)}, u32[]{:S(2)}) %collective-permute-start.1) | collective-permute-done | bytes 245792 | tf_op jit(solution)/shard_map/ppermute | solution.py:486
  24.2 0.2 pack_halo.1
  24.4 1.4 %collective-permute-start.2 = (f32[11,64,128]{2,1,0:T(8,128)S(1)}, f32[11,64,128]{2,1,0:T(8,128)S(1)}, u32[]{:S(2)}, u32[]{:S(2)}) collective-permute-start(f32[11,64,128]{2,1,0:T(8,128)S(1)} %get-tuple-element.22), channel_id=1, source_target_pairs={{0,1},{2,3},{4,5},{6,7},{8,9},{10,11},{12,13},{14,15},{16,17},{18,... | collective-permute-start | bytes 1081352 | tf_op jit(solution)/shard_map/ppermute | solution.py:486
  25.8 5.7 %collective-permute-start.3 = (f32[11,64,128]{2,1,0:T(8,128)S(1)}, f32[11,64,128]{2,1,0:T(8,128)S(1)}, u32[]{:S(2)}, u32[]{:S(2)}) collective-permute-start(f32[11,64,128]{2,1,0:T(8,128)S(1)} %get-tuple-element.23), channel_id=1, source_target_pairs={{1,2},{3,4},{5,6},{7,8},{9,10},{11,12},{13,14},{15,16},{17,18},{19... | collective-permute-start | bytes 1081352 | tf_op jit(solution)/shard_map/ppermute | solution.py:486
  31.5 9.9 %middle_rows.1 = (f32[16,128,128]{2,1,0:T(8,128)S(1)}, f32[64,64,128]{2,1,0:T(8,128)}) custom-call(bf16[32,128,256]{2,1,0:T(8,128)(2,1)S(1)} %get-tuple-element.15.refs_0_, bf16[32,128,128]{2,1,0:T(8,128)(2,1)S(1)} %get-tuple-element.16.refs_1_, bf16[11,128,128]{2,1,0:T(8,128)(2,1)S(1)} %copy-done, bf16[11,128,128]{2,1,0:T(8,128)(2,1)S(1)} %copy-done.1, ...), custom_call_target="tpu_custom_call" | custom-call | flops 8000000000 | bytes 8000000 | tf_op jit(solution)/shard_map/middle_rows/pallas_call | solution.py:383
  41.4 0.0 collective-permute-done.2.y_near
  41.4 1.3 %collective-permute-done.3.y_next = f32[11,64,128]{2,1,0:T(8,128)S(1)} collective-permute-done((f32[11,64,128]{2,1,0:T(8,128)S(1)}, f32[11,64,128]{2,1,0:T(8,128)S(1)}, u32[]{:S(2)}, u32[]{:S(2)}) %collective-permute-start.3) | collective-permute-done | bytes 360480 | tf_op jit(solution)/shard_map/ppermute | solution.py:486
  42.7 1.4 %merge_rows.1 = f32[64,64,128]{2,1,0:T(8,128)} custom-call(f32[16,128,128]{2,1,0:T(8,128)S(1)} %get-tuple-element.20.edge, f32[11,64,128]{2,1,0:T(8,128)S(1)} %collective-permute-done.2.y_near, f32[11,64,128]{2,1,0:T(8,128)S(1)} %collective-permute-done.3.y_next, f32[64,64,128]{2,1,0:T(8,128)} %get-tuple-element.24._), custom_call_target="tpu_custom_call", output_to_operand_aliasing={{}: (3, {})} | custom-call | tf_op jit(solution)/shard_map/merge_rows/pallas_call | solution.py:463
Async XLA Ops:
  1.9 13.4 %copy-start = (bf16[11,128,128]{2,1,0:T(8,128)(2,1)S(1)}, bf16[11,128,128]{2,1,0:T(8,128)(2,1)}, u32[]{:S(2)}) copy-start(bf16[11,128,128]{2,1,0:T(8,128)(2,1)} %constant.6.clone.band_z.refs_2_) | copy-start | bytes 1081348
  2.0 13.4 %copy-start.1 = (bf16[11,128,128]{2,1,0:T(8,128)(2,1)S(1)}, bf16[11,128,128]{2,1,0:T(8,128)(2,1)}, u32[]{:S(2)}) copy-start(bf16[11,128,128]{2,1,0:T(8,128)(2,1)} %constant.7.clone.refs_3_) | copy-start | bytes 1081348
  11.7 11.2 %collective-permute-start = (f32[480,128]{1,0:T(8,128)S(1)}, f32[480,128]{1,0:T(8,128)S(1)}, u32[]{:S(2)}, u32[]{:S(2)}) collective-permute-start(f32[480,128]{1,0:T(8,128)S(1)} %get-tuple-element.18), channel_id=1, source_target_pairs={{0,32},{64,96},{128,160},{192,224},{32,0},{96,64},{160,128},{224,1... | collective-permute-start | bytes 737288 | tf_op jit(solution)/shard_map/ppermute | solution.py:486
  13.4 10.8 %collective-permute-start.1 = (f32[480,128]{1,0:T(8,128)S(1)}, f32[480,128]{1,0:T(8,128)S(1)}, u32[]{:S(2)}, u32[]{:S(2)}) collective-permute-start(f32[480,128]{1,0:T(8,128)S(1)} %get-tuple-element.19), channel_id=1, source_target_pairs={{32,64},{96,128},{160,192},{64,32},{128,96},{192,160},{33,65},{97,... | collective-permute-start | bytes 737288 | tf_op jit(solution)/shard_map/ppermute | solution.py:486
  24.4 17.0 %collective-permute-start.2 = (f32[11,64,128]{2,1,0:T(8,128)S(1)}, f32[11,64,128]{2,1,0:T(8,128)S(1)}, u32[]{:S(2)}, u32[]{:S(2)}) collective-permute-start(f32[11,64,128]{2,1,0:T(8,128)S(1)} %get-tuple-element.22), channel_id=1, source_target_pairs={{0,1},{2,3},{4,5},{6,7},{8,9},{10,11},{12,13},{14,15},{16,17},{18,... | collective-permute-start | bytes 1081352 | tf_op jit(solution)/shard_map/ppermute | solution.py:486
  25.8 16.8 %collective-permute-start.3 = (f32[11,64,128]{2,1,0:T(8,128)S(1)}, f32[11,64,128]{2,1,0:T(8,128)S(1)}, u32[]{:S(2)}, u32[]{:S(2)}) collective-permute-start(f32[11,64,128]{2,1,0:T(8,128)S(1)} %get-tuple-element.23), channel_id=1, source_target_pairs={{1,2},{3,4},{5,6},{7,8},{9,10},{11,12},{13,14},{15,16},{17,18},{19... | collective-permute-start | bytes 1081352 | tf_op jit(solution)/shard_map/ppermute | solution.py:486

commit v6 on v5

--- a/solution.py
+++ b/solution.py
@@ -17,7 +17,7 @@
 PART = HALF // 2
 REACHED = PART + MARGIN
 RIM = 16
-RIM_AHEAD = 4
+RIM_AHEAD = 11
 MAIN_AHEAD = 2
 MAIN_SLOTS = 4
 HALO_ROWS = 480
@@ -493,12 +493,12 @@
     source, reach, x_near, x_next = rim(
         (brick_class, sharpness, threshold), fields, in_hbm(band_z), in_hbm(band_rim)
     )
+    x_near = swapped(x_near, "gx", 0)
     x_next = swapped(x_next, "gx", 1)
-    x_near = swapped(x_near, "gx", 0)
     halo, partial = spread_rows(0, source, reach, band_z, band_x)
     y_near, y_next = pack(halo, x_near, x_next)
+    y_near = swapped(y_near, "gy", 0)
     y_next = swapped(y_next, "gy", 1)
-    y_near = swapped(y_near, "gy", 0)
     edge, out = spread_rows(1, source, reach, band_z, band_x, partial, x_near, x_next)
     return merge(edge, y_near, y_next, out)
 

time: 44.4 us -> 44.1 us (level)
  transfers between devices with their start and end apart: 4 -> 4, of which waited for: 2 -> 2; matrix products, arithmetic and copies ran while one was open for 0% -> 0% of each run, Pallas kernels for 39% -> 40%
where the time goes in v6:
time: 44.1 us; the launch traced here: 44 us
  Pallas kernels  28.5 us (65%)
  starting transfers between devices  10.7 us (24%)
  waiting for transfers between devices  2.52 us (6%)
  between operations  2.19 us (5%)
    pallas_call x2, Pallas kernels, spread_rows(): pl.pallas_call(functools.partial(rows_kernel, part), grid=(steps,), out_s...  17.4 us
    ppermute x4, starting transfers between devices, swapped(): return lax.ppermute(value, axis, pairs + [(b, a) for a, b in pairs])  10.7 us
    pallas_call x1, Pallas kernels, rim(): pl.pallas_call(rim_kernel, grid=(groups + 1,), out_shape=[jax.ShapeDtypeS...  9.42 us
    ppermute x4, waiting for transfers between devices, swapped(): return lax.ppermute(value, axis, pairs + [(b, a) for a, b in pairs])  2.52 us
    pallas_call x1, Pallas kernels, merge(): pl.pallas_call(merge_kernel, grid=(PART // GROUP,), out_shape=jax.ShapeDt...  1.43 us
  transfers between devices with their start and end apart: 4, of which 2 were waited for; matrix products, arithmetic and copies ran while one was open for 0% of the time, Pallas kernels for 40%

profile of v6, /device:TPU:91, one launch (start us, length us, event | category | flops | bytes accessed | tf_op | source)
XLA Modules:
  0.0 44.0 jit_solution(11310535413300147619)
XLA Ops:
  1.9 0.0 copy-start
  2.0 0.0 copy-start.1
  2.0 9.4 %source_and_rim.1 = (bf16[32,128,256]{2,1,0:T(8,128)(2,1)S(1)}, bf16[32,128,128]{2,1,0:T(8,128)(2,1)S(1)}, f32[480,128]{1,0:T(8,128)S(1)}, f32[480,128]{1,0:T(8,128)S(1)}) custom-call(s32[1,1]{1,0:T(1,128)S(6)} %copy.12.class_ref, f32[1]{0:T(128)S(6)} %copy.13.sharp_ref, f32[1]{0:T(128)S(6)} %copy.14.thresh_ref, f32[64,64,128]{2,1,0:T(8,128)} %fil1.1, ...), custom_call_target="tpu_custom_call" | custom-call | flops 4000000000 | bytes 11000000 | tf_op jit(solution)/shard_map/source_and_rim/pallas_call | solution.py:220
  11.4 1.7 %collective-permute-start = (f32[480,128]{1,0:T(8,128)S(1)}, f32[480,128]{1,0:T(8,128)S(1)}, u32[]{:S(2)}, u32[]{:S(2)}) collective-permute-start(f32[480,128]{1,0:T(8,128)S(1)} %get-tuple-element.18), channel_id=1, source_target_pairs={{0,32},{64,96},{128,160},{192,224},{32,0},{96,64},{160,128},{224,1... | collective-permute-start | bytes 737288 | tf_op jit(solution)/shard_map/ppermute | solution.py:486
  13.1 1.9 %collective-permute-start.1 = (f32[480,128]{1,0:T(8,128)S(1)}, f32[480,128]{1,0:T(8,128)S(1)}, u32[]{:S(2)}, u32[]{:S(2)}) collective-permute-start(f32[480,128]{1,0:T(8,128)S(1)} %get-tuple-element.19), channel_id=1, source_target_pairs={{32,64},{96,128},{160,192},{64,32},{128,96},{192,160},{33,65},{97,... | collective-permute-start | bytes 737288 | tf_op jit(solution)/shard_map/ppermute | solution.py:486
  15.0 0.0 copy-done
  15.0 0.0 copy-done.1
  15.1 7.6 %edge_rows.1 = (f32[11,128,128]{2,1,0:T(8,128)S(1)}, f32[27,128,128]{2,1,0:T(8,128)S(1)}) custom-call(bf16[32,128,256]{2,1,0:T(8,128)(2,1)S(1)} %get-tuple-element.15.refs_0_, bf16[32,128,128]{2,1,0:T(8,128)(2,1)S(1)} %get-tuple-element.16.refs_1_, bf16[11,128,128]{2,1,0:T(8,128)(2,1)S(1)} %copy-done, bf16[11,128,128]{2,1,0:T(8,128)(2,1)S(1)} %copy-done.1), custom_call_target="tpu_custom_call" | custom-call | flops 8000000000 | bytes 8000000 | tf_op jit(solution)/shard_map/edge_rows/pallas_call | solution.py:383
  22.6 0.0 collective-permute-done.refs_5_.x_near
  22.6 1.3 %collective-permute-done.1.refs_6_.x_next = f32[480,128]{1,0:T(8,128)S(1)} collective-permute-done((f32[480,128]{1,0:T(8,128)S(1)}, f32[480,128]{1,0:T(8,128)S(1)}, u32[]{:S(2)}, u32[]{:S(2)}) %collective-permute-start.1) | collective-permute-done | bytes 245792 | tf_op jit(solution)/shard_map/ppermute | solution.py:486
  23.9 0.2 pack_halo.1
  24.1 1.4 %collective-permute-start.2 = (f32[11,64,128]{2,1,0:T(8,128)S(1)}, f32[11,64,128]{2,1,0:T(8,128)S(1)}, u32[]{:S(2)}, u32[]{:S(2)}) collective-permute-start(f32[11,64,128]{2,1,0:T(8,128)S(1)} %get-tuple-element.22), channel_id=1, source_target_pairs={{0,1},{2,3},{4,5},{6,7},{8,9},{10,11},{12,13},{14,15},{16,17},{18,... | collective-permute-start | bytes 1081352 | tf_op jit(solution)/shard_map/ppermute | solution.py:486
  25.6 5.7 %collective-permute-start.3 = (f32[11,64,128]{2,1,0:T(8,128)S(1)}, f32[11,64,128]{2,1,0:T(8,128)S(1)}, u32[]{:S(2)}, u32[]{:S(2)}) collective-permute-start(f32[11,64,128]{2,1,0:T(8,128)S(1)} %get-tuple-element.23), channel_id=1, source_target_pairs={{1,2},{3,4},{5,6},{7,8},{9,10},{11,12},{13,14},{15,16},{17,18},{19... | collective-permute-start | bytes 1081352 | tf_op jit(solution)/shard_map/ppermute | solution.py:486
  31.2 9.9 %middle_rows.1 = (f32[16,128,128]{2,1,0:T(8,128)S(1)}, f32[64,64,128]{2,1,0:T(8,128)}) custom-call(bf16[32,128,256]{2,1,0:T(8,128)(2,1)S(1)} %get-tuple-element.15.refs_0_, bf16[32,128,128]{2,1,0:T(8,128)(2,1)S(1)} %get-tuple-element.16.refs_1_, bf16[11,128,128]{2,1,0:T(8,128)(2,1)S(1)} %copy-done, bf16[11,128,128]{2,1,0:T(8,128)(2,1)S(1)} %copy-done.1, ...), custom_call_target="tpu_custom_call" | custom-call | flops 8000000000 | bytes 8000000 | tf_op jit(solution)/shard_map/middle_rows/pallas_call | solution.py:383
  41.1 0.0 collective-permute-done.2.y_near
  41.1 1.2 %collective-permute-done.3.y_next = f32[11,64,128]{2,1,0:T(8,128)S(1)} collective-permute-done((f32[11,64,128]{2,1,0:T(8,128)S(1)}, f32[11,64,128]{2,1,0:T(8,128)S(1)}, u32[]{:S(2)}, u32[]{:S(2)}) %collective-permute-start.3) | collective-permute-done | bytes 360480 | tf_op jit(solution)/shard_map/ppermute | solution.py:486
  42.4 1.4 %merge_rows.1 = f32[64,64,128]{2,1,0:T(8,128)} custom-call(f32[16,128,128]{2,1,0:T(8,128)S(1)} %get-tuple-element.20.edge, f32[11,64,128]{2,1,0:T(8,128)S(1)} %collective-permute-done.2.y_near, f32[11,64,128]{2,1,0:T(8,128)S(1)} %collective-permute-done.3.y_next, f32[64,64,128]{2,1,0:T(8,128)} %get-tuple-element.24._), custom_call_target="tpu_custom_call", output_to_operand_aliasing={{}: (3, {})} | custom-call | tf_op jit(solution)/shard_map/merge_rows/pallas_call | solution.py:463
Async XLA Ops:
  1.9 13.1 %copy-start = (bf16[11,128,128]{2,1,0:T(8,128)(2,1)S(1)}, bf16[11,128,128]{2,1,0:T(8,128)(2,1)}, u32[]{:S(2)}) copy-start(bf16[11,128,128]{2,1,0:T(8,128)(2,1)} %constant.6.clone.band_z.refs_2_) | copy-start | bytes 1081348
  2.0 13.1 %copy-start.1 = (bf16[11,128,128]{2,1,0:T(8,128)(2,1)S(1)}, bf16[11,128,128]{2,1,0:T(8,128)(2,1)}, u32[]{:S(2)}) copy-start(bf16[11,128,128]{2,1,0:T(8,128)(2,1)} %constant.7.clone.refs_3_) | copy-start | bytes 1081348
  11.4 11.2 %collective-permute-start = (f32[480,128]{1,0:T(8,128)S(1)}, f32[480,128]{1,0:T(8,128)S(1)}, u32[]{:S(2)}, u32[]{:S(2)}) collective-permute-start(f32[480,128]{1,0:T(8,128)S(1)} %get-tuple-element.18), channel_id=1, source_target_pairs={{0,32},{64,96},{128,160},{192,224},{32,0},{96,64},{160,128},{224,1... | collective-permute-start | bytes 737288 | tf_op jit(solution)/shard_map/ppermute | solution.py:486
  13.1 10.8 %collective-permute-start.1 = (f32[480,128]{1,0:T(8,128)S(1)}, f32[480,128]{1,0:T(8,128)S(1)}, u32[]{:S(2)}, u32[]{:S(2)}) collective-permute-start(f32[480,128]{1,0:T(8,128)S(1)} %get-tuple-element.19), channel_id=1, source_target_pairs={{32,64},{96,128},{160,192},{64,32},{128,96},{192,160},{33,65},{97,... | collective-permute-start | bytes 737288 | tf_op jit(solution)/shard_map/ppermute | solution.py:486
  24.1 17.0 %collective-permute-start.2 = (f32[11,64,128]{2,1,0:T(8,128)S(1)}, f32[11,64,128]{2,1,0:T(8,128)S(1)}, u32[]{:S(2)}, u32[]{:S(2)}) collective-permute-start(f32[11,64,128]{2,1,0:T(8,128)S(1)} %get-tuple-element.22), channel_id=1, source_target_pairs={{0,1},{2,3},{4,5},{6,7},{8,9},{10,11},{12,13},{14,15},{16,17},{18,... | collective-permute-start | bytes 1081352 | tf_op jit(solution)/shard_map/ppermute | solution.py:486
  25.6 16.8 %collective-permute-start.3 = (f32[11,64,128]{2,1,0:T(8,128)S(1)}, f32[11,64,128]{2,1,0:T(8,128)S(1)}, u32[]{:S(2)}, u32[]{:S(2)}) collective-permute-start(f32[11,64,128]{2,1,0:T(8,128)S(1)} %get-tuple-element.23), channel_id=1, source_target_pairs={{1,2},{3,4},{5,6},{7,8},{9,10},{11,12},{13,14},{15,16},{17,18},{19... | collective-permute-start | bytes 1081352 | tf_op jit(solution)/shard_map/ppermute | solution.py:486
